TPU v7x, 32 devices: a whole 2x2x4 slice. The times are simulated.
32 devices in a mesh: groups: 2 (over y), dom: 4 (over z), rep: 4 (over x, core).
Axes of the slice: x: 2, y: 2, z: 4, core: 2. Of those that a mesh axis runs over, the one named last changes fastest.
Arguments:
- plan: int32 [4], P('dom'), may hold values from 0 to 3, as said below
- edge_lhs: int32 [8, 4096], P(('groups', 'dom'), 'rep'), parts along dimension 0, may hold values from 0 to 511
- edge_rhs: int32 [8, 4096], P(('groups', 'dom'), 'rep'), parts along dimension 0, may hold values from 0 to 255
- edge_rel: int32 [8, 4096], P(('groups', 'dom'), 'rep'), parts along dimension 0, may hold values from 0 to 511
- edge_count: int32 [32], P(('groups', 'dom', 'rep')), parts along dimension 0, may hold values from 1 to 1024, 8192 in all
- negatives: int32 [8, 8, 1000], P(('groups', 'dom'), 'rep'), parts along dimension 0, may hold values from 0 to 255
- emb: float32 [2048, 400], P(('groups', 'dom')), parts along dimension 0, may hold values from -2.4 to 2.4
- acc: float32 [2048], P(('groups', 'dom')), parts along dimension 0, may hold values from 0.2 to 2
- hot_emb: float32 [512, 400], P('groups'), parts along dimension 0, may hold values from -2.4 to 2.4
- hot_acc: float32 [512], P('groups'), parts along dimension 0, may hold values from 4 to 40
- relations: float32 [1024, 400], P('groups'), parts along dimension 0, may hold values from -4.2 to 4.2
Outputs:
- new_emb: float32 [2048, 400], P(('groups', 'dom')), parts along dimension 0
- new_acc: float32 [2048], P(('groups', 'dom')), parts along dimension 0
- new_hot: float32 [512, 400], P('groups'), parts along dimension 0
- new_hot_acc: float32 [512], P('groups'), parts along dimension 0
There are 2 independent parts, one for each index of `groups`. A program takes and returns all parts, laid end to end along the dimension named above; an argument that names none is the same for every part. Nothing has to cross between parts.
Inputs may be any that keep to these rules, and one draw needn't show every extreme that they name: Worker w trains its own partition against partition plan[w] = (w + s) mod 4, for one s of 1 to 3 common to all workers and all groups. `edge_lhs`: values below 256 name rows of the worker's own partition, the others hot entity value - 256. `edge_count`: the live slots of a list come first. `negatives`: rows of the planned partition, repeats allowed.
All inputs are finite; a program needn't handle non-finite values. No bound on the sum of `edge_count` on one device may be relied on, other than what follows from the above.
Results may differ from a plain program's by a relative error of at most 0.004.
Values may be sent and summed in bfloat16 or wider, within the bound.
No kernel may reach another device: no remote copies, remote signals or barrier semaphores. Data moves between devices by JAX's collectives and lax.ppermute only.
A program may use at most 64 MiB of HBM per device.

v0:
```python
import functools

import jax
import jax.numpy as jnp
from jax import lax
from jax.experimental import pallas as pl
from jax.experimental.pallas import tpu as pltpu
from jax.sharding import PartitionSpec as P

LEARN_RATE = 0.5
BF = jnp.bfloat16
F32 = jnp.float32
LHS, RHS, REL, NEG, LIVE = 0, 1, 2, 3, 5
VMEM_LIMIT = 24 * 1024 * 1024


def call(kernel, out_shape, n_in, scratch=(), anywhere=(), smem=()):
    spaces = [
        pltpu.SMEM if i in smem else pl.ANY if i in anywhere else pltpu.VMEM for i in range(n_in)
    ]
    return pl.pallas_call(
        kernel,
        out_shape=out_shape,
        in_specs=[pl.BlockSpec(memory_space=space) for space in spaces],
        scratch_shapes=list(scratch),
        compiler_params=pltpu.CompilerParams(vmem_limit_bytes=VMEM_LIMIT),
        cost_estimate=pl.CostEstimate(flops=1, bytes_accessed=1, transcendentals=0),
    )


def dot_nt(a, b):
    return lax.dot_general(a, b, (((1,), (1,)), ((), ())), preferred_element_type=F32)


def dot_nn(a, b):
    return jnp.dot(a, b, preferred_element_type=F32)


def one_hot(ids, count):
    rows = lax.broadcasted_iota(jnp.int32, (count, ids.shape[1]), 0).astype(jnp.int16)
    return jnp.where(rows == ids.astype(jnp.int16), jnp.ones((), BF), jnp.zeros((), BF))


def fetch_all(pairs, sems):
    copies = [
        pltpu.make_async_copy(src, dst, sems.at[i]) for i, (src, dst) in enumerate(pairs)
    ]
    for copy in copies:
        copy.start()
    return copies


def halves(axis_size):
    core = lax.axis_index("rep") % 2
    cut = axis_size // 2
    return [pl.ds(pl.multiple_of(c * cut, cut), cut) for c in (core, 1 - core)]


def pack_kernel(count, emb, lhs, rhs, rel, neg, half, ids):
    half[...] = emb[:, halves(emb.shape[1])[0]].astype(BF)
    width = ids.shape[1]
    ids[...] = jnp.full(ids.shape, -1, jnp.int32)
    ids[LHS : LHS + 1, :] = lhs[...]
    ids[RHS : RHS + 1, :] = rhs[...]
    ids[REL : REL + 1, :] = rel[...]
    ids[NEG : NEG + 2, 0 : neg.shape[2]] = neg[0]
    ids[LIVE : LIVE + 1, :] = jnp.full((1, width), count[0], jnp.int32)


def count_rows(ids, counts):
    spans, rows, _ = counts.shape
    for b in range(spans):
        named = ids[NEG + b : NEG + b + 1, :]
        row_ids = lax.broadcasted_iota(jnp.int32, (rows, 128), 0)
        times = jnp.zeros((rows, 128), F32)
        for start in range(0, named.shape[1], 128):
            times += jnp.where(row_ids == named[:, start : start + 128], 1.0, 0.0)
        counts[b] = jnp.broadcast_to(jnp.sum(times, axis=1, keepdims=True), times.shape)


def list_columns(ids, table, rel_parts, query, rel_cols):
    spans, width, per = query.shape
    half = width // 2
    n_rel = rel_parts.shape[1] // 2
    rel_hot = one_hot(ids[REL : REL + 1, :], n_rel)
    rel_all = dot_nn(rel_parts[:, :n_rel], rel_hot) + dot_nn(rel_parts[:, n_rel:], rel_hot)
    left_all = dot_nn(table[...], one_hot(ids[LHS : LHS + 1, :], table.shape[1]))
    for b in range(spans):
        lanes = slice(b * per, (b + 1) * per)
        left, rel_col = left_all[:, lanes], rel_all[:, lanes]
        rel_cols[b] = rel_col
        l_re, l_im = left[:half], left[half:]
        r_re, r_im = rel_col[:half], rel_col[half:]
        query[b, :half] = (l_re * r_re - l_im * r_im).astype(BF)
        query[b, half:] = (l_re * r_im + l_im * r_re).astype(BF)


def first_kernel(
    emb, hot, rel, ids, table, rel_parts, query, rel_cols, counts, emb_s, hot_s, rel_s, sems
):
    copies = fetch_all([(emb, emb_s), (hot, hot_s), (rel, rel_s)], sems)
    count_rows(ids, counts)
    rows = emb.shape[1]
    copies[0].wait()
    table[:, :rows] = emb_s[...].astype(BF)
    copies[1].wait()
    table[:, rows:] = hot_s[...].astype(BF)
    copies[2].wait()
    n_rel = rel.shape[1]
    high = rel_s[...].astype(BF)
    rel_parts[:, :n_rel] = high
    rel_parts[:, n_rel:] = (rel_s[...] - high.astype(F32)).astype(BF)
    list_columns(ids, table, rel_parts, query, rel_cols)


def second_kernel(table, rel_parts, ids, query, rel_cols, counts):
    count_rows(ids, counts)
    list_columns(ids, table, rel_parts, query, rel_cols)


def relay_kernel(one, after, other, out):
    del after, other
    out[...] = one[...]


def edges_kernel(n_negs, far_half, far_rest, *refs):
    lists = (refs[0:4], refs[4:8])
    lefts, keep, send, far, *totals = refs[8:]
    mine, theirs = halves(far.shape[1])
    far[:, mine] = far_half[...]
    far[:, theirs] = far_rest[...]
    rows = far.shape[1]
    hot_rows = totals[0].shape[1]
    far_t = far[...].astype(F32).T.astype(BF)
    work = []
    for i, (ids, query, rel_cols, counts) in enumerate(lists):
        for b in range(query.shape[0]):
            work.append((i, b, dot_nn(far_t, query[b])))
    spans, width, per = lists[0][1].shape
    half = width // 2
    row_ids = lax.broadcasted_iota(jnp.int32, (rows, per), 0)
    done = []
    for i, b, scores in work:
        ids, query, rel_cols, counts = lists[i]
        lanes = slice(b * per, (b + 1) * per)
        right = row_ids == ids[RHS : RHS + 1, lanes]
        place = lax.broadcasted_iota(jnp.int32, (1, per), 1) + b * per
        mask = jnp.where(place < ids[LIVE : LIVE + 1, lanes], 1.0, 0.0)
        chance = 0.5 * jnp.tanh(0.5 * scores) + 0.5
        times = jnp.concatenate([counts[b]] * (per // 128), axis=1)
        grad = (chance * (mask / n_negs)).astype(BF).astype(F32) * times
        grad = (grad + jnp.where(right, (chance - 1.0) * mask, 0.0)).astype(BF)
        done.append((i, b, grad))
    for i, b, grad in done:
        ids, query, rel_cols, counts = lists[i]
        at = i * spans + b
        lanes = slice(b * per, (b + 1) * per)
        gq = dot_nn(far[...], grad)
        r_re, r_im = rel_cols[b, :half], rel_cols[b, half:]
        g_re, g_im = gq[:half], gq[half:]
        lefts[at, :half] = (g_re * r_re + g_im * r_im).astype(BF)
        lefts[at, half:] = (g_im * r_re - g_re * r_im).astype(BF)
        add_far = dot_nt(query[b], grad)
        hot_total, far_total = totals[2 * i : 2 * i + 2]
        if b == 0:
            far_total[...] = add_far
        else:
            far_total[...] += add_far
    for i, b, grad in done:
        ids, query, rel_cols, counts = lists[i]
        at = i * spans + b
        lanes = slice(b * per, (b + 1) * per)
        hot_total, far_total = totals[2 * i : 2 * i + 2]
        left_hot = one_hot(ids[LHS : LHS + 1, lanes] - rows, hot_rows)
        add_hot = dot_nt(lefts[at], left_hot)
        if b == 0:
            hot_total[...] = add_hot
        else:
            hot_total[...] += add_hot
    cut = hot_rows // 2
    for j, (mine, theirs) in enumerate((halves(hot_rows), halves(rows))):
        lanes = slice(0, cut) if j == 0 else slice(cut, cut + rows // 2)
        keep[:, lanes] = totals[j][:, mine] + totals[2 + j][:, mine]
        send[:, lanes] = (totals[j][:, theirs] + totals[2 + j][:, theirs]).astype(BF)


def own_kernel(ids_0, ids_1, lefts, far_in, keep, send, far, *totals):
    far[...] = far_in[...]
    per = lefts.shape[2]
    rows = totals[0].shape[1]
    for i, ids in enumerate((ids_0, ids_1)):
        spans = lefts.shape[0] // 2
        for b in range(spans):
            left_own = one_hot(ids[LHS : LHS + 1, b * per : (b + 1) * per], rows)
            add = dot_nt(lefts[i * spans + b], left_own)
            if b == 0:
                totals[i][...] = add
            else:
                totals[i][...] += add
    mine, theirs = halves(rows)
    keep[...] = totals[0][:, mine] + totals[1][:, mine]
    send[...] = (totals[0][:, theirs] + totals[1][:, theirs]).astype(BF)


def pair_kernel(keep, got, hot, far):
    cut = hot.shape[1]
    hot[...] = (keep[:, :cut] + got[:, :cut].astype(F32)).astype(BF)
    part = far.shape[0]
    at = pl.ds(pl.multiple_of(lax.axis_index("rep") // 2 * (hot.shape[0] - part), 16), part)
    far[...] = (keep[at, cut:] + got[at, cut:].astype(F32)).astype(BF)


def add_kernel(one, other, out):
    out[...] = (one[...].astype(F32) + other[...].astype(F32)).astype(BF)


def own_sum_kernel(keep, got, far, far_other, out):
    first = lax.axis_index("rep") // 2 == 0
    low = jnp.where(first, far[...].astype(F32), far_other[...].astype(F32))
    high = jnp.where(first, far_other[...].astype(F32), far[...].astype(F32))
    part = low.shape[0]
    over = 2 * part - out.shape[0]
    total = keep[...] + got[...].astype(F32)
    out[:part] = total[:part] + low
    out[part:] = total[part:] + high[over:]


def whole_kernel(own, one, other, out):
    cut = own.shape[1]
    out[:, :cut] = own[...]
    out[:, cut:] = one[...].astype(F32) + other[...].astype(F32)


def adagrad(weights, accum, grad):
    new = accum + jnp.sum(grad * grad, axis=0, keepdims=True) / grad.shape[0]
    return weights - LEARN_RATE * grad / jnp.sqrt(new), new


def near_update_kernel(grads, emb, acc, hot, hot_acc, done, done_acc, rest, rest_acc):
    cut = grads.shape[1] // 2
    mine, theirs = halves(2 * cut)
    for i, (w, a) in enumerate(((emb, acc), (hot, hot_acc))):
        lanes = slice(i * cut, (i + 1) * cut)
        done[:, lanes], done_acc[:, lanes] = adagrad(w[:, mine], a[:, mine], grads[:, lanes])
        rest[:, lanes] = w[:, theirs]
        rest_acc[:, lanes] = a[:, theirs]


def far_update_kernel(grads, done, done_acc, rest, rest_acc, emb, acc, hot, hot_acc):
    cut = grads.shape[1] // 2
    mine, theirs = halves(2 * cut)
    for i, (w, a) in enumerate(((emb, acc), (hot, hot_acc))):
        lanes = slice(i * cut, (i + 1) * cut)
        w[:, mine] = done[:, lanes]
        a[:, mine] = done_acc[:, lanes]
        w[:, theirs], a[:, theirs] = adagrad(rest[:, lanes], rest_acc[:, lanes], grads[:, lanes])


def shifted(block, axis, distance):
    size = lax.axis_size(axis)
    return lax.ppermute(block, axis, [((i - distance) % size, i) for i in range(size)])


def swapped(block, bit):
    return lax.ppermute(block, "rep", [(i, i ^ bit) for i in range(lax.axis_size("rep"))])


def struct(shape, dtype):
    return jax.ShapeDtypeStruct(shape, dtype)


def bucket(fetch, home, count, lhs, rhs, rel_ids, neg, emb, hot, rel):
    width, rows = emb.shape
    hot_rows = hot.shape[1]
    edges = lhs.shape[1]
    spans, n_negs = neg.shape[1:]
    per = edges // spans
    blocks = 2 * spans
    emb_half, ids = call(
        pack_kernel,
        (struct((width, rows // 2), BF), struct((8, edges), jnp.int32)),
        n_in=6,
        smem=(0,),
    )(count, emb, lhs, rhs, rel_ids, neg)
    far_half = fetch(emb_half)
    other = swapped(ids, 2)
    columns = (
        struct((spans, width, per), BF),
        struct((spans, width, per), F32),
        struct((spans, rows, 128), F32),
    )
    table, rel_parts, *mine = call(
        first_kernel,
        (struct((width, rows + hot_rows), BF), struct((width, 2 * rel.shape[1]), BF), *columns),
        n_in=4,
        anywhere=(0, 1, 2),
        scratch=[pltpu.VMEM(x.shape, F32) for x in (emb, hot, rel)] + [pltpu.SemaphoreType.DMA((3,))],
    )(emb, hot, rel, ids)
    far_half = call(relay_kernel, struct(far_half.shape, BF), n_in=3, anywhere=(1, 2))(
        far_half, table, other
    )
    far_rest = swapped(far_half, 1)
    theirs = call(second_kernel, columns, n_in=3)(table, rel_parts, other)
    hot_half = struct((width, hot_rows // 2), BF)
    row_half = struct((width, rows // 2), BF)
    both = (width, hot_rows // 2 + rows // 2)
    lefts, keep, send = call(
        functools.partial(edges_kernel, n_negs),
        (struct((blocks, width, per), BF), struct(both, F32), struct(both, BF)),
        scratch=[pltpu.VMEM((width, rows), BF)]
        + [pltpu.VMEM((width, hot_rows), F32), pltpu.VMEM((width, rows), F32)] * 2,
        n_in=10,
    )(far_half, far_rest, ids, *mine, other, *theirs)
    part = struct((-(-width // 32) * 16, rows // 2), BF)
    hot_sum, far_sum = call(pair_kernel, (hot_half, part), n_in=2)(keep, swapped(send, 1))
    own_keep, own_send, far_sum = call(
        own_kernel,
        (struct(row_half.shape, F32), row_half, part),
        scratch=[pltpu.VMEM((width, rows), F32)] * 2,
        n_in=4,
    )(ids, other, lefts, far_sum)
    arrived = home(far_sum)
    arrived_other = swapped(arrived, 2)
    own_got = swapped(own_send, 1)
    size = lax.axis_size("dom")
    for digit in range(size.bit_length() - 1):
        if digit > 0:
            hot_sum = call(add_kernel, hot_half, n_in=2)(hot_sum, hot_got)
        route = [(i, i ^ (1 << digit)) for i in range(size)]
        hot_got = lax.ppermute(hot_sum, "dom", route)
    own = call(own_sum_kernel, struct(row_half.shape, F32), n_in=4)(
        own_keep, own_got, arrived, arrived_other
    )
    return call(whole_kernel, struct((width, rows // 2 + hot_rows // 2), F32), n_in=3)(
        own, hot_sum, hot_got
    )


def four_workers(offset, arrays):
    def branch(shift):
        return functools.partial(
            bucket,
            lambda block: shifted(block, "dom", -shift),
            lambda block: shifted(block, "dom", shift),
        )

    return lax.switch(offset - 1, [branch(1), branch(2), branch(3)], *arrays)


def digit_set(offset, digit):
    return offset // (1 << digit) % 2 == 1


def many_workers(offset, arrays):
    size = lax.axis_size("dom")
    digits = size.bit_length() - 1

    def moved(block, sign):
        for digit in range(digits):
            block = jnp.where(
                digit_set(offset, digit), shifted(block, "dom", sign * (1 << digit)), block
            )
        return block

    return bucket(
        lambda block: moved(block, -1), lambda block: moved(block, 1), *arrays
    )


def body(
    plan, edge_lhs, edge_rhs, edge_rel, edge_count, negatives, emb, acc, hot_emb, hot_acc, relations
):
    emb, acc, hot, hot_acc, rel = emb.T, acc[None, :], hot_emb.T, hot_acc[None, :], relations.T
    workers = lax.axis_size("dom")
    offset = (plan[0] - lax.axis_index("dom")) % workers
    run = four_workers if workers == 4 else many_workers
    mine = run(offset, (edge_count, edge_lhs, edge_rhs, edge_rel, negatives, emb, hot, rel))
    theirs = swapped(mine, 1)
    half, half_acc = struct(mine.shape, F32), struct((1, mine.shape[1]), F32)
    ready = call(near_update_kernel, (half, half_acc, half, half_acc), n_in=5)(
        mine, emb, acc, hot, hot_acc
    )
    new_emb, new_acc, new_hot, new_hot_acc = call(
        far_update_kernel, tuple(struct(x.shape, F32) for x in (emb, acc, hot, hot_acc)), n_in=5
    )(theirs, *ready)
    return (new_emb.T, new_acc[0], new_hot.T, new_hot_acc[0])


def solution(mesh):
    placed = (
        P("dom"),
        P(("groups", "dom"), "rep"),
        P(("groups", "dom"), "rep"),
        P(("groups", "dom"), "rep"),
        P(("groups", "dom", "rep")),
        P(("groups", "dom"), "rep", None),
        P(("groups", "dom"), None),
        P(("groups", "dom")),
        P("groups", None),
        P("groups"),
        P("groups", None),
    )
    return jax.shard_map(
        body,
        mesh=mesh,
        in_specs=placed,
        out_specs=(
            P(("groups", "dom"), None),
            P(("groups", "dom")),
            P("groups", None),
            P("groups"),
        ),
        check_vma=False,
    )
```

profile of v0, /device:TPU:0, one launch (start us, length us, event | category | flops | bytes accessed | tf_op | source)
XLA Modules:
  0.0 34.7 jit_solution(9743091734280921121)
XLA Ops:
  1.3 30.6 %conditional.1 = (f32[400,256]{1,0:T(8,128)S(1)}) conditional(s32[]{:T(128)} %clamp.3, (s32[1]{0:T(128)}, f32[400,256]{1,0:T(8,128)}, s32[1,1024]{1,0:T(1,128)}, s32[1,1024]{1,0:T(1,128)}, s32[1,1024]{1,0:T(1,128)}, /*index=5*/s32[1,2,1000]{2,1,0:T(2,128)}, f32[400,256]{1,0:T(8,128)}, f32[400,512]{1,0:T(8,128)}) %tuple.28, ...), branch_computations={%region_0.1_spmd, %region_1.2_spmd, %region_2.3_spmd} | conditional | flops 10 | bytes 3424634 | solution.py:347
  1.3 1.7 %branch_0_fun.10 = (bf16[400,128]{1,0:T(8,128)(2,1)S(1)}, s32[8,1024]{1,0:T(8,128)S(1)}) custom-call(s32[1]{0:T(128)} %get-tuple-element.38.count, f32[400,256]{1,0:T(8,128)} %get-tuple-element.39.emb, s32[1,1024]{1,0:T(1,128)} %get-tuple-element.54.lhs, s32[1,1024]{1,0:T(1,128)} %get-tuple-element.55.rhs, s32[1,1024]{1,0:T(1,128)} %get-tuple-element.56.rel, ...), custom_call_target="tpu_custom_call" | custom-call | flops 1 | bytes 1 | tf_op jit(solution)/shard_map/cond/branch_0_fun/pallas_call | solution.py:279
  3.0 5.1 %collective-permute-start.1 = (bf16[400,128]{1,0:T(8,128)(2,1)S(1)}, bf16[400,128]{1,0:T(8,128)(2,1)S(1)}, u32[]{:S(2)}, u32[]{:S(2)}) collective-permute-start(bf16[400,128]{1,0:T(8,128)(2,1)S(1)} %get-tuple-element.59), channel_id=1, source_target_pairs={{4,0},{8,4},{12,8},{0,12},{5,1},{9,5},{13,9},{1,13},{6,2},{10,6},{... | collective-permute-start | bytes 307208 | tf_op jit(solution)/shard_map/cond/branch_0_fun/ppermute | solution.py:261
  8.1 1.5 %collective-permute-start = (s32[8,1024]{1,0:T(8,128)S(1)}, s32[8,1024]{1,0:T(8,128)S(1)}, u32[]{:S(2)}, u32[]{:S(2)}) collective-permute-start(s32[8,1024]{1,0:T(8,128)S(1)} %get-tuple-element.58.ids.refs_0_.ids_0), channel_id=1, source_target_pairs={{0,2},{1,3},{2,0},{3,1},{4,6},{5,7},{6,4},{7,5},{8,10},{9,11},{10,... | collective-permute-start | bytes 98312 | tf_op jit(solution)/shard_map/cond/branch_0_fun/ppermute | solution.py:265
  9.6 3.0 %branch_0_fun.11 = (bf16[400,512]{1,0:T(8,128)(2,1)S(1)}, bf16[400,1024]{1,0:T(8,128)(2,1)S(1)}, bf16[2,400,512]{2,1,0:T(8,128)(2,1)S(1)}, f32[2,400,512]{2,1,0:T(8,128)S(1)}, f32[2,256,128]{2,1,0:T(8,128)S(1)}) custom-call(f32[400,256]{1,0:T(8,128)} %get-tuple-element.39.emb, f32[400,256]{1,0:T(8,128)} %get-tuple-element.60.hot, ...), custom_call_target="tpu_custom_call" | custom-call | flops 1 | bytes 1 | tf_op jit(solution)/shard_map/cond/branch_0_fun/pallas_call | solution.py:292
  12.7 0.1 collective-permute-start.2
  12.7 1.7 %branch_0_fun.13 = (bf16[2,400,512]{2,1,0:T(8,128)(2,1)S(1)}, f32[2,400,512]{2,1,0:T(8,128)S(1)}, f32[2,256,128]{2,1,0:T(8,128)S(1)}) custom-call(bf16[400,512]{1,0:T(8,128)(2,1)S(1)} %get-tuple-element.62.after.table, bf16[400,1024]{1,0:T(8,128)(2,1)S(1)} %get-tuple-element.66.rel_parts, s32[8,1024]{1,0:T(8,128)S(1)} %collective-permute-done.other.ids.refs_4_.ids_1), custom_call_target="tpu_custom_call" | custom-call | flops 1 | bytes 1 | tf_op jit(solution)/shard_map/cond/branch_0_fun/pallas_call | solution.py:303
  14.4 2.8 %branch_0_fun.14 = (bf16[4,400,512]{2,1,0:T(8,128)(2,1)S(1)}, f32[400,256]{1,0:T(8,128)S(1)}, bf16[400,256]{1,0:T(8,128)(2,1)S(1)}) custom-call(bf16[400,128]{1,0:T(8,128)(2,1)S(1)} %branch_0_fun.12.far_half, bf16[400,128]{1,0:T(8,128)(2,1)S(1)} %collective-permute-done.2.far_rest, s32[8,1024]{1,0:T(8,128)S(1)} %get-tuple-element.58.ids.refs_0_.ids_0, ...), custom_call_target="tpu_custom_call" | custom-call | flops 1 | bytes 1 | tf_op jit(solution)/shard_map/cond/branch_0_fun/pallas_call | solution.py:307
  17.2 0.6 %collective-permute-start.3 = (bf16[400,256]{1,0:T(8,128)(2,1)S(1)}, bf16[400,256]{1,0:T(8,128)(2,1)S(1)}, u32[]{:S(2)}, u32[]{:S(2)}) collective-permute-start(bf16[400,256]{1,0:T(8,128)(2,1)S(1)} %get-tuple-element.72), channel_id=1, source_target_pairs={{0,1},{1,0},{2,3},{3,2},{4,5},{5,4},{6,7},{7,6},{8,9},{9,8},{10,11... | collective-permute-start | bytes 614408 | tf_op jit(solution)/shard_map/cond/branch_0_fun/ppermute | solution.py:265
  17.8 1.1 %collective-permute-done.3.got = bf16[400,256]{1,0:T(8,128)(2,1)S(1)} collective-permute-done((bf16[400,256]{1,0:T(8,128)(2,1)S(1)}, bf16[400,256]{1,0:T(8,128)(2,1)S(1)}, u32[]{:S(2)}, u32[]{:S(2)}) %collective-permute-start.3) | collective-permute-done | bytes 204832 | tf_op jit(solution)/shard_map/cond/branch_0_fun/ppermute | solution.py:265
  18.9 0.1 collective-permute-start.7
  19.0 0.7 %branch_0_fun.16 = (f32[400,128]{1,0:T(8,128)S(1)}, bf16[400,128]{1,0:T(8,128)(2,1)S(1)}, bf16[208,128]{1,0:T(8,128)(2,1)S(1)}) custom-call(s32[8,1024]{1,0:T(8,128)S(1)} %get-tuple-element.58.ids.refs_0_.ids_0, s32[8,1024]{1,0:T(8,128)S(1)} %collective-permute-done.other.ids.refs_4_.ids_1, bf16[4,400,512]{2,1,0:T(8,128)(2,1)S(1)} %get-tuple-element.70.lefts, ...), custom_call_target="tpu_custom_call" | custom-call | flops 1 | bytes 1 | tf_op jit(solution)/shard_map/cond/branch_0_fun/pallas_call | solution.py:316
  19.7 2.1 %collective-permute-start.5 = (bf16[208,128]{1,0:T(8,128)(2,1)S(1)}, bf16[208,128]{1,0:T(8,128)(2,1)S(1)}, u32[]{:S(2)}, u32[]{:S(2)}) collective-permute-start(bf16[208,128]{1,0:T(8,128)(2,1)S(1)} %get-tuple-element.76), channel_id=1, source_target_pairs={{12,0},{0,4},{4,8},{8,12},{13,1},{1,5},{5,9},{9,13},{14,2},{2,6},{... | collective-permute-start | bytes 159752 | tf_op jit(solution)/shard_map/cond/branch_0_fun/ppermute | solution.py:261
  21.8 2.4 %collective-permute-done.7.other = bf16[400,128]{1,0:T(8,128)(2,1)S(1)} collective-permute-done((bf16[400,128]{1,0:T(8,128)(2,1)S(1)}, bf16[400,128]{1,0:T(8,128)(2,1)S(1)}, u32[]{:S(2)}, u32[]{:S(2)}) %collective-permute-start.7) | collective-permute-done | bytes 102432 | tf_op jit(solution)/shard_map/cond/branch_0_fun/ppermute | solution.py:330
  24.2 0.9 %collective-permute-start.8 = (bf16[400,128]{1,0:T(8,128)(2,1)S(1)}, bf16[400,128]{1,0:T(8,128)(2,1)S(1)}, u32[]{:S(2)}, u32[]{:S(2)}) collective-permute-start(bf16[400,128]{1,0:T(8,128)(2,1)S(1)} %branch_0_fun.18.one), channel_id=1, source_target_pairs={{0,8},{4,12},{8,0},{12,4},{1,9},{5,13},{9,1},{13,5},{2,10},{6,14},... | collective-permute-start | bytes 307208 | tf_op jit(solution)/shard_map/cond/branch_0_fun/ppermute | solution.py:330
  25.0 0.7 %collective-permute-done.5.far = bf16[208,128]{1,0:T(8,128)(2,1)S(1)} collective-permute-done((bf16[208,128]{1,0:T(8,128)(2,1)S(1)}, bf16[208,128]{1,0:T(8,128)(2,1)S(1)}, u32[]{:S(2)}, u32[]{:S(2)}) %collective-permute-start.5) | collective-permute-done | bytes 53280 | tf_op jit(solution)/shard_map/cond/branch_0_fun/ppermute | solution.py:261
  25.7 1.3 %collective-permute-start.6 = (bf16[208,128]{1,0:T(8,128)(2,1)S(1)}, bf16[208,128]{1,0:T(8,128)(2,1)S(1)}, u32[]{:S(2)}, u32[]{:S(2)}) collective-permute-start(bf16[208,128]{1,0:T(8,128)(2,1)S(1)} %collective-permute-done.5.far), channel_id=1, source_target_pairs={{0,2},{1,3},{2,0},{3,1},{4,6},{5,7},{6,4},{7,5},{8,10},{9,11},{10,... | collective-permute-start | bytes 159752 | tf_op jit(solution)/shard_map/cond/branch_0_fun/ppermute | solution.py:265
  27.0 2.8 %collective-permute-done.6.far_other = bf16[208,128]{1,0:T(8,128)(2,1)S(1)} collective-permute-done((bf16[208,128]{1,0:T(8,128)(2,1)S(1)}, bf16[208,128]{1,0:T(8,128)(2,1)S(1)}, u32[]{:S(2)}, u32[]{:S(2)}) %collective-permute-start.6) | collective-permute-done | bytes 53280 | tf_op jit(solution)/shard_map/cond/branch_0_fun/ppermute | solution.py:265
  29.8 0.1 branch_0_fun.17.own
  29.9 1.8 %collective-permute-done.8.other = bf16[400,128]{1,0:T(8,128)(2,1)S(1)} collective-permute-done((bf16[400,128]{1,0:T(8,128)(2,1)S(1)}, bf16[400,128]{1,0:T(8,128)(2,1)S(1)}, u32[]{:S(2)}, u32[]{:S(2)}) %collective-permute-start.8) | collective-permute-done | bytes 102432 | tf_op jit(solution)/shard_map/cond/branch_0_fun/ppermute | solution.py:330
  31.9 0.1 collective-permute-start.27
  32.0 1.3 %shard_map.138 = (f32[400,256]{1,0:T(8,128)S(1)}, f32[1,256]{1,0:T(1,128)S(1)}, f32[400,256]{1,0:T(8,128)S(1)}, f32[1,256]{1,0:T(1,128)S(1)}) custom-call(f32[400,256]{1,0:T(8,128)S(1)} %get-tuple-element.150.grads, f32[400,256]{1,0:T(8,128)} %bitcast.16, f32[1,256]{1,0:T(1,128)S(1)} %bitcast.11, f32[400,256]{1,0:T(8,128)} %bitcast.23, f32[1,256]{1,0:T(1,128)S(1)} %bitcast.12), custom_call_target="tpu_custom_call" | custom-call | flops 1 | bytes 1 | tf_op jit(solution)/shard_map/pallas_call | solution.py:380
  33.3 0.4 %collective-permute-done.27.grads = f32[400,256]{1,0:T(8,128)S(1)} collective-permute-done((f32[400,256]{1,0:T(8,128)S(1)}, f32[400,256]{1,0:T(8,128)S(1)}, u32[]{:S(2)}, u32[]{:S(2)}) %collective-permute-start.27) | collective-permute-done | bytes 409632 | tf_op jit(solution)/shard_map/ppermute | solution.py:265
  33.7 1.0 %shard_map.139 = (f32[400,256]{1,0:T(8,128)}, f32[1,256]{1,0:T(1,128)}, f32[400,256]{1,0:T(8,128)}, f32[1,256]{1,0:T(1,128)}) custom-call(f32[400,256]{1,0:T(8,128)S(1)} %collective-permute-done.27.grads, f32[400,256]{1,0:T(8,128)S(1)} %get-tuple-element.142.done, f32[1,256]{1,0:T(1,128)S(1)} %get-tuple-element.143.done_acc, ...), custom_call_target="tpu_custom_call" | custom-call | flops 1 | bytes 1 | tf_op jit(solution)/shard_map/pallas_call | solution.py:383
  (13 shorter events, 0.1 us)
Async XLA Ops:
  1.3 30.7 %copy-start = (f32[256]{0:T(256)S(1)}, f32[256]{0:T(256)}, u32[]{:S(2)}) copy-start(f32[256]{0:T(256)} %param.21) | copy-start | bytes 3076
  1.3 30.7 %copy-start.1 = (f32[256]{0:T(256)S(1)}, f32[256]{0:T(256)}, u32[]{:S(2)}) copy-start(f32[256]{0:T(256)} %param.23) | copy-start | bytes 3076
  3.0 9.6 %collective-permute-start.1 = (bf16[400,128]{1,0:T(8,128)(2,1)S(1)}, bf16[400,128]{1,0:T(8,128)(2,1)S(1)}, u32[]{:S(2)}, u32[]{:S(2)}) collective-permute-start(bf16[400,128]{1,0:T(8,128)(2,1)S(1)} %get-tuple-element.59), channel_id=1, source_target_pairs={{4,0},{8,4},{12,8},{0,12},{5,1},{9,5},{13,9},{1,13},{6,2},{10,6},{... | collective-permute-start | bytes 307208 | tf_op jit(solution)/shard_map/cond/branch_0_fun/ppermute | solution.py:261
  8.1 4.5 %collective-permute-start = (s32[8,1024]{1,0:T(8,128)S(1)}, s32[8,1024]{1,0:T(8,128)S(1)}, u32[]{:S(2)}, u32[]{:S(2)}) collective-permute-start(s32[8,1024]{1,0:T(8,128)S(1)} %get-tuple-element.58.ids.refs_0_.ids_0), channel_id=1, source_target_pairs={{0,2},{1,3},{2,0},{3,1},{4,6},{5,7},{6,4},{7,5},{8,10},{9,11},{10,... | collective-permute-start | bytes 98312 | tf_op jit(solution)/shard_map/cond/branch_0_fun/ppermute | solution.py:265
  12.7 1.8 %collective-permute-start.2 = (bf16[400,128]{1,0:T(8,128)(2,1)S(1)}, bf16[400,128]{1,0:T(8,128)(2,1)S(1)}, u32[]{:S(2)}, u32[]{:S(2)}) collective-permute-start(bf16[400,128]{1,0:T(8,128)(2,1)S(1)} %branch_0_fun.12.far_half), channel_id=1, source_target_pairs={{0,1},{1,0},{2,3},{3,2},{4,5},{5,4},{6,7},{7,6},{8,9},{9,8},{10,11... | collective-permute-start | bytes 307208 | tf_op jit(solution)/shard_map/cond/branch_0_fun/ppermute | solution.py:265
  17.2 1.6 %collective-permute-start.3 = (bf16[400,256]{1,0:T(8,128)(2,1)S(1)}, bf16[400,256]{1,0:T(8,128)(2,1)S(1)}, u32[]{:S(2)}, u32[]{:S(2)}) collective-permute-start(bf16[400,256]{1,0:T(8,128)(2,1)S(1)} %get-tuple-element.72), channel_id=1, source_target_pairs={{0,1},{1,0},{2,3},{3,2},{4,5},{5,4},{6,7},{7,6},{8,9},{9,8},{10,11... | collective-permute-start | bytes 614408 | tf_op jit(solution)/shard_map/cond/branch_0_fun/ppermute | solution.py:265
  18.9 5.2 %collective-permute-start.7 = (bf16[400,128]{1,0:T(8,128)(2,1)S(1)}, bf16[400,128]{1,0:T(8,128)(2,1)S(1)}, u32[]{:S(2)}, u32[]{:S(2)}) collective-permute-start(bf16[400,128]{1,0:T(8,128)(2,1)S(1)} %get-tuple-element.77.one), channel_id=1, source_target_pairs={{0,4},{4,0},{8,12},{12,8},{1,5},{5,1},{9,13},{13,9},{2,6},{6,2},{1... | collective-permute-start | bytes 307208 | tf_op jit(solution)/shard_map/cond/branch_0_fun/ppermute | solution.py:330
  19.7 6.0 %collective-permute-start.5 = (bf16[208,128]{1,0:T(8,128)(2,1)S(1)}, bf16[208,128]{1,0:T(8,128)(2,1)S(1)}, u32[]{:S(2)}, u32[]{:S(2)}) collective-permute-start(bf16[208,128]{1,0:T(8,128)(2,1)S(1)} %get-tuple-element.76), channel_id=1, source_target_pairs={{12,0},{0,4},{4,8},{8,12},{13,1},{1,5},{5,9},{9,13},{14,2},{2,6},{... | collective-permute-start | bytes 159752 | tf_op jit(solution)/shard_map/cond/branch_0_fun/ppermute | solution.py:261
  21.8 5.2 %collective-permute-start.4 = (bf16[400,128]{1,0:T(8,128)(2,1)S(1)}, bf16[400,128]{1,0:T(8,128)(2,1)S(1)}, u32[]{:S(2)}, u32[]{:S(2)}) collective-permute-start(bf16[400,128]{1,0:T(8,128)(2,1)S(1)} %get-tuple-element.75), channel_id=1, source_target_pairs={{0,1},{1,0},{2,3},{3,2},{4,5},{5,4},{6,7},{7,6},{8,9},{9,8},{10,11... | collective-permute-start | bytes 307208 | tf_op jit(solution)/shard_map/cond/branch_0_fun/ppermute | solution.py:265
  24.2 7.5 %collective-permute-start.8 = (bf16[400,128]{1,0:T(8,128)(2,1)S(1)}, bf16[400,128]{1,0:T(8,128)(2,1)S(1)}, u32[]{:S(2)}, u32[]{:S(2)}) collective-permute-start(bf16[400,128]{1,0:T(8,128)(2,1)S(1)} %branch_0_fun.18.one), channel_id=1, source_target_pairs={{0,8},{4,12},{8,0},{12,4},{1,9},{5,13},{9,1},{13,5},{2,10},{6,14},... | collective-permute-start | bytes 307208 | tf_op jit(solution)/shard_map/cond/branch_0_fun/ppermute | solution.py:330
  25.7 4.1 %collective-permute-start.6 = (bf16[208,128]{1,0:T(8,128)(2,1)S(1)}, bf16[208,128]{1,0:T(8,128)(2,1)S(1)}, u32[]{:S(2)}, u32[]{:S(2)}) collective-permute-start(bf16[208,128]{1,0:T(8,128)(2,1)S(1)} %collective-permute-done.5.far), channel_id=1, source_target_pairs={{0,2},{1,3},{2,0},{3,1},{4,6},{5,7},{6,4},{7,5},{8,10},{9,11},{10,... | collective-permute-start | bytes 159752 | tf_op jit(solution)/shard_map/cond/branch_0_fun/ppermute | solution.py:265
  31.9 1.8 %collective-permute-start.27 = (f32[400,256]{1,0:T(8,128)S(1)}, f32[400,256]{1,0:T(8,128)S(1)}, u32[]{:S(2)}, u32[]{:S(2)}) collective-permute-start(f32[400,256]{1,0:T(8,128)S(1)} %get-tuple-element.150.grads), channel_id=1, source_target_pairs={{0,1},{1,0},{2,3},{3,2},{4,5},{5,4},{6,7},{7,6},{8,9},{9,8},{10,11... | collective-permute-start | bytes 1228808 | tf_op jit(solution)/shard_map/ppermute | solution.py:265
where the time goes:
time: 34.4 us; the launch traced here: 34.7 us
  Pallas kernels  12.3 us (36%)
  starting transfers between devices  11.6 us (34%)
  waiting for transfers between devices  9.15 us (27%)
  between operations  1.34 us (4%)
    ppermute x2, starting transfers between devices, shifted(): lax.ppermute(block, axis, [((i - distance) % size, i) for i in range(size)])  7.18 us
    ppermute x6, waiting for transfers between devices, swapped(): lax.ppermute(block, 'rep', [(i, i ^ bit) for i in range(lax.axis_size('re...  4.36 us
    ppermute x2, waiting for transfers between devices, bucket(): hot_got = lax.ppermute(hot_sum, 'dom', route)  4.12 us
    ppermute x6, starting transfers between devices, swapped(): lax.ppermute(block, 'rep', [(i, i ^ bit) for i in range(lax.axis_size('re...  3.52 us
    pallas_call x1, Pallas kernels, bucket(): call(first_kernel, (struct((width, rows + hot_rows), BF), struct((width,...  2.97 us
    pallas_call x1, Pallas kernels, bucket(): call(functools.partial(edges_kernel, n_negs), (struct((blocks, width, per...  2.77 us
    pallas_call x1, Pallas kernels, bucket(): call(pack_kernel, (struct((width, rows // 2), BF), struct((8, edges), jnp...  1.71 us
    pallas_call x1, Pallas kernels, bucket(): theirs = call(second_kernel, columns, n_in=3)(table, rel_parts, other)  1.69 us
  transfers between devices with their start and end apart: 10, of which 6 were waited for; matrix products, arithmetic and copies ran while one was open for 0% of the time, Pallas kernels for 19%

commit v1 on v0

--- a/solution.py
+++ b/solution.py
@@ -41,30 +41,25 @@
     return jnp.where(rows == ids.astype(jnp.int16), jnp.ones((), BF), jnp.zeros((), BF))
 
 
-def fetch_all(pairs, sems):
-    copies = [
-        pltpu.make_async_copy(src, dst, sems.at[i]) for i, (src, dst) in enumerate(pairs)
-    ]
-    for copy in copies:
-        copy.start()
-    return copies
-
-
 def halves(axis_size):
     core = lax.axis_index("rep") % 2
     cut = axis_size // 2
     return [pl.ds(pl.multiple_of(c * cut, cut), cut) for c in (core, 1 - core)]
 
 
-def pack_kernel(count, emb, lhs, rhs, rel, neg, half, ids):
+def pack_kernel(emb, lhs, rhs, rel, neg, hot, relations, half, ids):
+    del hot, relations
     half[...] = emb[:, halves(emb.shape[1])[0]].astype(BF)
-    width = ids.shape[1]
     ids[...] = jnp.full(ids.shape, -1, jnp.int32)
     ids[LHS : LHS + 1, :] = lhs[...]
     ids[RHS : RHS + 1, :] = rhs[...]
     ids[REL : REL + 1, :] = rel[...]
     ids[NEG : NEG + 2, 0 : neg.shape[2]] = neg[0]
-    ids[LIVE : LIVE + 1, :] = jnp.full((1, width), count[0], jnp.int32)
+
+
+def live_kernel(count, ids, out):
+    out[...] = ids[...]
+    out[LIVE : LIVE + 1, :] = jnp.full((1, ids.shape[1]), count[0], jnp.int32)
 
 
 def count_rows(ids, counts):
@@ -95,21 +90,15 @@
         query[b, half:] = (l_re * r_im + l_im * r_re).astype(BF)
 
 
-def first_kernel(
-    emb, hot, rel, ids, table, rel_parts, query, rel_cols, counts, emb_s, hot_s, rel_s, sems
-):
-    copies = fetch_all([(emb, emb_s), (hot, hot_s), (rel, rel_s)], sems)
+def first_kernel(emb, hot, rel, ids, table, rel_parts, query, rel_cols, counts):
     count_rows(ids, counts)
     rows = emb.shape[1]
-    copies[0].wait()
-    table[:, :rows] = emb_s[...].astype(BF)
-    copies[1].wait()
-    table[:, rows:] = hot_s[...].astype(BF)
-    copies[2].wait()
+    table[:, :rows] = emb[...].astype(BF)
+    table[:, rows:] = hot[...].astype(BF)
     n_rel = rel.shape[1]
-    high = rel_s[...].astype(BF)
+    high = rel[...].astype(BF)
     rel_parts[:, :n_rel] = high
-    rel_parts[:, n_rel:] = (rel_s[...] - high.astype(F32)).astype(BF)
+    rel_parts[:, n_rel:] = (rel[...] - high.astype(F32)).astype(BF)
     list_columns(ids, table, rel_parts, query, rel_cols)
 
 
@@ -279,10 +268,11 @@
     emb_half, ids = call(
         pack_kernel,
         (struct((width, rows // 2), BF), struct((8, edges), jnp.int32)),
-        n_in=6,
-        smem=(0,),
-    )(count, emb, lhs, rhs, rel_ids, neg)
+        n_in=7,
+        anywhere=(5, 6),
+    )(emb, lhs, rhs, rel_ids, neg, hot, rel)
     far_half = fetch(emb_half)
+    ids = call(live_kernel, struct(ids.shape, jnp.int32), n_in=2, smem=(0,))(count, ids)
     other = swapped(ids, 2)
     columns = (
         struct((spans, width, per), BF),
@@ -293,8 +283,6 @@
         first_kernel,
         (struct((width, rows + hot_rows), BF), struct((width, 2 * rel.shape[1]), BF), *columns),
         n_in=4,
-        anywhere=(0, 1, 2),
-        scratch=[pltpu.VMEM(x.shape, F32) for x in (emb, hot, rel)] + [pltpu.SemaphoreType.DMA((3,))],
     )(emb, hot, rel, ids)
     far_half = call(relay_kernel, struct(far_half.shape, BF), n_in=3, anywhere=(1, 2))(
         far_half, table, other

time: 34.4 us -> 34 us (0.988)
  Pallas kernels: 12.3 us -> 11.2 us
  waiting for transfers between devices: 9.15 us -> 9.81 us
    pallas_call x1, Pallas kernels: 2.97 us -> 1.7 us  [bucket(): call(first_kernel, (struct((width, rows + hot_rows), BF), struct((width,...]
    pallas_call x0 -> x1, Pallas kernels: none -> 0.65 us  [bucket(): call(live_kernel, struct(ids.shape, jnp.int32), n_in=2, smem=(0,))]
    pallas_call x1, Pallas kernels: 1.71 us -> 1.18 us  [bucket(): call(pack_kernel, (struct((width, rows // 2), BF), struct((8, edges), jnp...]
    ppermute x6, waiting for transfers between devices: 4.36 us -> 4.88 us  [swapped(): lax.ppermute(block, 'rep', [(i, i ^ bit) for i in range(lax.axis_size('re...]
  transfers between devices with their start and end apart: 10 -> 10, of which waited for: 6 -> 7; matrix products, arithmetic and copies ran while one was open for 0% -> 0% of each run, Pallas kernels for 19% -> 18%
where the time goes in v1:
time: 34 us; the launch traced here: 34.4 us
  starting transfers between devices  11.7 us (34%)
  Pallas kernels  11.2 us (33%)
  waiting for transfers between devices  9.81 us (29%)
  between operations  1.34 us (4%)
  loops' own time  0.35 us (1%)
    ppermute x2, starting transfers between devices, shifted(): lax.ppermute(block, axis, [((i - distance) % size, i) for i in range(size)])  7.18 us
    ppermute x6, waiting for transfers between devices, swapped(): lax.ppermute(block, 'rep', [(i, i ^ bit) for i in range(lax.axis_size('re...  4.88 us
    ppermute x2, waiting for transfers between devices, bucket(): hot_got = lax.ppermute(hot_sum, 'dom', route)  4.12 us
    ppermute x6, starting transfers between devices, swapped(): lax.ppermute(block, 'rep', [(i, i ^ bit) for i in range(lax.axis_size('re...  3.77 us
    pallas_call x1, Pallas kernels, bucket(): call(functools.partial(edges_kernel, n_negs), (struct((blocks, width, per...  2.8 us
    pallas_call x1, Pallas kernels, bucket(): call(first_kernel, (struct((width, rows + hot_rows), BF), struct((width,...  1.7 us
    pallas_call x1, Pallas kernels, bucket(): theirs = call(second_kernel, columns, n_in=3)(table, rel_parts, other)  1.69 us
    pallas_call x1, Pallas kernels, body(): call(near_update_kernel, (half, half_acc, half, half_acc), n_in=5)  1.26 us
  transfers between devices with their start and end apart: 10, of which 7 were waited for; matrix products, arithmetic and copies ran while one was open for 0% of the time, Pallas kernels for 18%

profile of v1, /device:TPU:0, one launch (start us, length us, event | category | flops | bytes accessed | tf_op | source)
XLA Modules:
  0.0 34.4 jit_solution(10531250355841486186)
XLA Ops:
  1.3 30.3 %conditional.1 = (f32[400,256]{1,0:T(8,128)S(1)}) conditional(s32[]{:T(128)} %clamp.3, (f32[400,256]{1,0:T(8,128)}, s32[1,1024]{1,0:T(1,128)}, s32[1,1024]{1,0:T(1,128)}, s32[1,1024]{1,0:T(1,128)}, s32[1,2,1000]{2,1,0:T(2,128)}, /*index=5*/f32[400,256]{1,0:T(8,128)}, f32[400,512]{1,0:T(8,128)}, s32[1]{0:T(128)}) %tuple.28, ...), branch_computations={%region_0.1_spmd, %region_1.2_spmd, %region_2.3_spmd} | conditional | flops 11 | bytes 9978319 | solution.py:335
  1.4 1.2 %branch_0_fun.11 = (bf16[400,128]{1,0:T(8,128)(2,1)S(1)}, s32[8,1024]{1,0:T(8,128)S(1)}) custom-call(f32[400,256]{1,0:T(8,128)} %get-tuple-element.39.emb, s32[1,1024]{1,0:T(1,128)} %get-tuple-element.54.lhs, s32[1,1024]{1,0:T(1,128)} %get-tuple-element.55.rhs, s32[1,1024]{1,0:T(1,128)} %get-tuple-element.56.rel, s32[1,2,1000]{2,1,0:T(2,128)} %get-tuple-element.57.neg, ...), custom_call_target="tpu_custom_call" | custom-call | flops 1 | bytes 1 | tf_op jit(solution)/shard_map/cond/branch_0_fun/pallas_call | solution.py:268
  2.6 5.1 %collective-permute-start.1 = (bf16[400,128]{1,0:T(8,128)(2,1)S(1)}, bf16[400,128]{1,0:T(8,128)(2,1)S(1)}, u32[]{:S(2)}, u32[]{:S(2)}) collective-permute-start(bf16[400,128]{1,0:T(8,128)(2,1)S(1)} %get-tuple-element.61), channel_id=1, source_target_pairs={{4,0},{8,4},{12,8},{0,12},{5,1},{9,5},{13,9},{1,13},{6,2},{10,6},{... | collective-permute-start | bytes 307208 | tf_op jit(solution)/shard_map/cond/branch_0_fun/ppermute | solution.py:250
  7.7 0.6 %branch_0_fun.12.ids.refs_0_.ids_0 = s32[8,1024]{1,0:T(8,128)S(1)} custom-call(s32[1]{0:T(128)} %get-tuple-element.38.count, s32[8,1024]{1,0:T(8,128)S(1)} %get-tuple-element.60.ids), custom_call_target="tpu_custom_call" | custom-call | flops 1 | bytes 1 | tf_op jit(solution)/shard_map/cond/branch_0_fun/pallas_call | solution.py:275
  8.3 1.6 %collective-permute-start = (s32[8,1024]{1,0:T(8,128)S(1)}, s32[8,1024]{1,0:T(8,128)S(1)}, u32[]{:S(2)}, u32[]{:S(2)}) collective-permute-start(s32[8,1024]{1,0:T(8,128)S(1)} %branch_0_fun.12.ids.refs_0_.ids_0), channel_id=1, source_target_pairs={{0,2},{1,3},{2,0},{3,1},{4,6},{5,7},{6,4},{7,5},{8,10},{9,11},{10,... | collective-permute-start | bytes 98312 | tf_op jit(solution)/shard_map/cond/branch_0_fun/ppermute | solution.py:254
  9.9 1.7 %branch_0_fun.13 = (bf16[400,512]{1,0:T(8,128)(2,1)S(1)}, bf16[400,1024]{1,0:T(8,128)(2,1)S(1)}, bf16[2,400,512]{2,1,0:T(8,128)(2,1)S(1)}, f32[2,400,512]{2,1,0:T(8,128)S(1)}, f32[2,256,128]{2,1,0:T(8,128)S(1)}) custom-call(f32[400,256]{1,0:T(8,128)S(1)} %copy-done.5, f32[400,256]{1,0:T(8,128)S(1)} %copy-done.8, f32[400,512]{1,0:T(8,128)S(1)} %copy-done.2, ...), custom_call_target="tpu_custom_call" | custom-call | flops 1 | bytes 1 | tf_op jit(solution)/shard_map/cond/branch_0_fun/pallas_call | solution.py:282
  11.6 0.7 %collective-permute-done.other.ids.refs_4_.ids_1 = s32[8,1024]{1,0:T(8,128)S(1)} collective-permute-done((s32[8,1024]{1,0:T(8,128)S(1)}, s32[8,1024]{1,0:T(8,128)S(1)}, u32[]{:S(2)}, u32[]{:S(2)}) %collective-permute-start) | collective-permute-done | bytes 32800 | tf_op jit(solution)/shard_map/cond/branch_0_fun/ppermute | solution.py:254
  12.3 0.1 collective-permute-start.2
  12.4 1.7 %branch_0_fun.15 = (bf16[2,400,512]{2,1,0:T(8,128)(2,1)S(1)}, f32[2,400,512]{2,1,0:T(8,128)S(1)}, f32[2,256,128]{2,1,0:T(8,128)S(1)}) custom-call(bf16[400,512]{1,0:T(8,128)(2,1)S(1)} %get-tuple-element.62.after.table, bf16[400,1024]{1,0:T(8,128)(2,1)S(1)} %get-tuple-element.66.rel_parts, s32[8,1024]{1,0:T(8,128)S(1)} %collective-permute-done.other.ids.refs_4_.ids_1), custom_call_target="tpu_custom_call" | custom-call | flops 1 | bytes 1 | tf_op jit(solution)/shard_map/cond/branch_0_fun/pallas_call | solution.py:291
  14.1 2.8 %branch_0_fun.16 = (bf16[4,400,512]{2,1,0:T(8,128)(2,1)S(1)}, f32[400,256]{1,0:T(8,128)S(1)}, bf16[400,256]{1,0:T(8,128)(2,1)S(1)}) custom-call(bf16[400,128]{1,0:T(8,128)(2,1)S(1)} %branch_0_fun.14.far_half, bf16[400,128]{1,0:T(8,128)(2,1)S(1)} %collective-permute-done.2.far_rest, s32[8,1024]{1,0:T(8,128)S(1)} %branch_0_fun.12.ids.refs_0_.ids_0, ...), custom_call_target="tpu_custom_call" | custom-call | flops 1 | bytes 1 | tf_op jit(solution)/shard_map/cond/branch_0_fun/pallas_call | solution.py:295
  16.9 0.6 %collective-permute-start.3 = (bf16[400,256]{1,0:T(8,128)(2,1)S(1)}, bf16[400,256]{1,0:T(8,128)(2,1)S(1)}, u32[]{:S(2)}, u32[]{:S(2)}) collective-permute-start(bf16[400,256]{1,0:T(8,128)(2,1)S(1)} %get-tuple-element.72), channel_id=1, source_target_pairs={{0,1},{1,0},{2,3},{3,2},{4,5},{5,4},{6,7},{7,6},{8,9},{9,8},{10,11... | collective-permute-start | bytes 614408 | tf_op jit(solution)/shard_map/cond/branch_0_fun/ppermute | solution.py:254
  17.5 1.1 %collective-permute-done.3.got = bf16[400,256]{1,0:T(8,128)(2,1)S(1)} collective-permute-done((bf16[400,256]{1,0:T(8,128)(2,1)S(1)}, bf16[400,256]{1,0:T(8,128)(2,1)S(1)}, u32[]{:S(2)}, u32[]{:S(2)}) %collective-permute-start.3) | collective-permute-done | bytes 204832 | tf_op jit(solution)/shard_map/cond/branch_0_fun/ppermute | solution.py:254
  18.7 0.7 %branch_0_fun.18 = (f32[400,128]{1,0:T(8,128)S(1)}, bf16[400,128]{1,0:T(8,128)(2,1)S(1)}, bf16[208,128]{1,0:T(8,128)(2,1)S(1)}) custom-call(s32[8,1024]{1,0:T(8,128)S(1)} %branch_0_fun.12.ids.refs_0_.ids_0, s32[8,1024]{1,0:T(8,128)S(1)} %collective-permute-done.other.ids.refs_4_.ids_1, bf16[4,400,512]{2,1,0:T(8,128)(2,1)S(1)} %get-tuple-element.70.lefts, ...), custom_call_target="tpu_custom_call" | custom-call | flops 1 | bytes 1 | tf_op jit(solution)/shard_map/cond/branch_0_fun/pallas_call | solution.py:304
  19.4 2.1 %collective-permute-start.5 = (bf16[208,128]{1,0:T(8,128)(2,1)S(1)}, bf16[208,128]{1,0:T(8,128)(2,1)S(1)}, u32[]{:S(2)}, u32[]{:S(2)}) collective-permute-start(bf16[208,128]{1,0:T(8,128)(2,1)S(1)} %get-tuple-element.76), channel_id=1, source_target_pairs={{12,0},{0,4},{4,8},{8,12},{13,1},{1,5},{5,9},{9,13},{14,2},{2,6},{... | collective-permute-start | bytes 159752 | tf_op jit(solution)/shard_map/cond/branch_0_fun/ppermute | solution.py:250
  21.4 2.4 %collective-permute-done.7.other = bf16[400,128]{1,0:T(8,128)(2,1)S(1)} collective-permute-done((bf16[400,128]{1,0:T(8,128)(2,1)S(1)}, bf16[400,128]{1,0:T(8,128)(2,1)S(1)}, u32[]{:S(2)}, u32[]{:S(2)}) %collective-permute-start.7) | collective-permute-done | bytes 102432 | tf_op jit(solution)/shard_map/cond/branch_0_fun/ppermute | solution.py:318
  23.8 0.7 %collective-permute-start.8 = (bf16[400,128]{1,0:T(8,128)(2,1)S(1)}, bf16[400,128]{1,0:T(8,128)(2,1)S(1)}, u32[]{:S(2)}, u32[]{:S(2)}) collective-permute-start(bf16[400,128]{1,0:T(8,128)(2,1)S(1)} %branch_0_fun.20.one), channel_id=1, source_target_pairs={{0,8},{4,12},{8,0},{12,4},{1,9},{5,13},{9,1},{13,5},{2,10},{6,14},... | collective-permute-start | bytes 307208 | tf_op jit(solution)/shard_map/cond/branch_0_fun/ppermute | solution.py:318
  24.5 0.8 %collective-permute-done.5.far = bf16[208,128]{1,0:T(8,128)(2,1)S(1)} collective-permute-done((bf16[208,128]{1,0:T(8,128)(2,1)S(1)}, bf16[208,128]{1,0:T(8,128)(2,1)S(1)}, u32[]{:S(2)}, u32[]{:S(2)}) %collective-permute-start.5) | collective-permute-done | bytes 53280 | tf_op jit(solution)/shard_map/cond/branch_0_fun/ppermute | solution.py:250
  25.4 1.5 %collective-permute-start.6 = (bf16[208,128]{1,0:T(8,128)(2,1)S(1)}, bf16[208,128]{1,0:T(8,128)(2,1)S(1)}, u32[]{:S(2)}, u32[]{:S(2)}) collective-permute-start(bf16[208,128]{1,0:T(8,128)(2,1)S(1)} %collective-permute-done.5.far), channel_id=1, source_target_pairs={{0,2},{1,3},{2,0},{3,1},{4,6},{5,7},{6,4},{7,5},{8,10},{9,11},{10,... | collective-permute-start | bytes 159752 | tf_op jit(solution)/shard_map/cond/branch_0_fun/ppermute | solution.py:254
  26.9 2.6 %collective-permute-done.6.far_other = bf16[208,128]{1,0:T(8,128)(2,1)S(1)} collective-permute-done((bf16[208,128]{1,0:T(8,128)(2,1)S(1)}, bf16[208,128]{1,0:T(8,128)(2,1)S(1)}, u32[]{:S(2)}, u32[]{:S(2)}) %collective-permute-start.6) | collective-permute-done | bytes 53280 | tf_op jit(solution)/shard_map/cond/branch_0_fun/ppermute | solution.py:254
  29.5 1.8 %collective-permute-done.8.other = bf16[400,128]{1,0:T(8,128)(2,1)S(1)} collective-permute-done((bf16[400,128]{1,0:T(8,128)(2,1)S(1)}, bf16[400,128]{1,0:T(8,128)(2,1)S(1)}, u32[]{:S(2)}, u32[]{:S(2)}) %collective-permute-start.8) | collective-permute-done | bytes 102432 | tf_op jit(solution)/shard_map/cond/branch_0_fun/ppermute | solution.py:318
  31.6 0.1 collective-permute-start.27
  31.7 1.3 %shard_map.138 = (f32[400,256]{1,0:T(8,128)S(1)}, f32[1,256]{1,0:T(1,128)S(1)}, f32[400,256]{1,0:T(8,128)S(1)}, f32[1,256]{1,0:T(1,128)S(1)}) custom-call(f32[400,256]{1,0:T(8,128)S(1)} %get-tuple-element.150.grads, f32[400,256]{1,0:T(8,128)} %bitcast.19, f32[1,256]{1,0:T(1,128)S(1)} %bitcast.11, f32[400,256]{1,0:T(8,128)} %bitcast.23, f32[1,256]{1,0:T(1,128)S(1)} %bitcast.12), custom_call_target="tpu_custom_call" | custom-call | flops 1 | bytes 1 | tf_op jit(solution)/shard_map/pallas_call | solution.py:368
  32.9 0.4 %collective-permute-done.27.grads = f32[400,256]{1,0:T(8,128)S(1)} collective-permute-done((f32[400,256]{1,0:T(8,128)S(1)}, f32[400,256]{1,0:T(8,128)S(1)}, u32[]{:S(2)}, u32[]{:S(2)}) %collective-permute-start.27) | collective-permute-done | bytes 409632 | tf_op jit(solution)/shard_map/ppermute | solution.py:254
  33.4 1.0 %shard_map.139 = (f32[400,256]{1,0:T(8,128)}, f32[1,256]{1,0:T(1,128)}, f32[400,256]{1,0:T(8,128)}, f32[1,256]{1,0:T(1,128)}) custom-call(f32[400,256]{1,0:T(8,128)S(1)} %collective-permute-done.27.grads, f32[400,256]{1,0:T(8,128)S(1)} %get-tuple-element.142.done, f32[1,256]{1,0:T(1,128)S(1)} %get-tuple-element.143.done_acc, ...), custom_call_target="tpu_custom_call" | custom-call | flops 1 | bytes 1 | tf_op jit(solution)/shard_map/pallas_call | solution.py:371
  (20 shorter events, 0.3 us)
Async XLA Ops:
  1.3 30.4 %copy-start = (f32[256]{0:T(256)S(1)}, f32[256]{0:T(256)}, u32[]{:S(2)}) copy-start(f32[256]{0:T(256)} %param.21) | copy-start | bytes 3076
  1.3 30.4 %copy-start.1 = (f32[256]{0:T(256)S(1)}, f32[256]{0:T(256)}, u32[]{:S(2)}) copy-start(f32[256]{0:T(256)} %param.23) | copy-start | bytes 3076
  1.3 8.5 %copy-start.2 = (f32[400,512]{1,0:T(8,128)S(1)}, f32[400,512]{1,0:T(8,128)}, u32[]{:S(2)}) copy-start(f32[400,512]{1,0:T(8,128)} %get-tuple-element.59.relations.rel) | copy-start | bytes 2457604 | tf_op jit(solution)/shard_map/cond
  1.3 8.5 %copy-start.5 = (f32[400,256]{1,0:T(8,128)S(1)}, f32[400,256]{1,0:T(8,128)}, u32[]{:S(2)}) copy-start(f32[400,256]{1,0:T(8,128)} %get-tuple-element.39.emb) | copy-start | bytes 1228804 | tf_op jit(solution)/shard_map/cond
  1.4 8.5 %copy-start.8 = (f32[400,256]{1,0:T(8,128)S(1)}, f32[400,256]{1,0:T(8,128)}, u32[]{:S(2)}) copy-start(f32[400,256]{1,0:T(8,128)} %get-tuple-element.58.hot) | copy-start | bytes 1228804 | tf_op jit(solution)/shard_map/cond
  2.6 9.7 %collective-permute-start.1 = (bf16[400,128]{1,0:T(8,128)(2,1)S(1)}, bf16[400,128]{1,0:T(8,128)(2,1)S(1)}, u32[]{:S(2)}, u32[]{:S(2)}) collective-permute-start(bf16[400,128]{1,0:T(8,128)(2,1)S(1)} %get-tuple-element.61), channel_id=1, source_target_pairs={{4,0},{8,4},{12,8},{0,12},{5,1},{9,5},{13,9},{1,13},{6,2},{10,6},{... | collective-permute-start | bytes 307208 | tf_op jit(solution)/shard_map/cond/branch_0_fun/ppermute | solution.py:250
  8.3 4.0 %collective-permute-start = (s32[8,1024]{1,0:T(8,128)S(1)}, s32[8,1024]{1,0:T(8,128)S(1)}, u32[]{:S(2)}, u32[]{:S(2)}) collective-permute-start(s32[8,1024]{1,0:T(8,128)S(1)} %branch_0_fun.12.ids.refs_0_.ids_0), channel_id=1, source_target_pairs={{0,2},{1,3},{2,0},{3,1},{4,6},{5,7},{6,4},{7,5},{8,10},{9,11},{10,... | collective-permute-start | bytes 98312 | tf_op jit(solution)/shard_map/cond/branch_0_fun/ppermute | solution.py:254
  12.3 1.8 %collective-permute-start.2 = (bf16[400,128]{1,0:T(8,128)(2,1)S(1)}, bf16[400,128]{1,0:T(8,128)(2,1)S(1)}, u32[]{:S(2)}, u32[]{:S(2)}) collective-permute-start(bf16[400,128]{1,0:T(8,128)(2,1)S(1)} %branch_0_fun.14.far_half), channel_id=1, source_target_pairs={{0,1},{1,0},{2,3},{3,2},{4,5},{5,4},{6,7},{7,6},{8,9},{9,8},{10,11... | collective-permute-start | bytes 307208 | tf_op jit(solution)/shard_map/cond/branch_0_fun/ppermute | solution.py:254
  16.9 1.6 %collective-permute-start.3 = (bf16[400,256]{1,0:T(8,128)(2,1)S(1)}, bf16[400,256]{1,0:T(8,128)(2,1)S(1)}, u32[]{:S(2)}, u32[]{:S(2)}) collective-permute-start(bf16[400,256]{1,0:T(8,128)(2,1)S(1)} %get-tuple-element.72), channel_id=1, source_target_pairs={{0,1},{1,0},{2,3},{3,2},{4,5},{5,4},{6,7},{7,6},{8,9},{9,8},{10,11... | collective-permute-start | bytes 614408 | tf_op jit(solution)/shard_map/cond/branch_0_fun/ppermute | solution.py:254
  18.6 5.2 %collective-permute-start.7 = (bf16[400,128]{1,0:T(8,128)(2,1)S(1)}, bf16[400,128]{1,0:T(8,128)(2,1)S(1)}, u32[]{:S(2)}, u32[]{:S(2)}) collective-permute-start(bf16[400,128]{1,0:T(8,128)(2,1)S(1)} %get-tuple-element.77.one), channel_id=1, source_target_pairs={{0,4},{4,0},{8,12},{12,8},{1,5},{5,1},{9,13},{13,9},{2,6},{6,2},{1... | collective-permute-start | bytes 307208 | tf_op jit(solution)/shard_map/cond/branch_0_fun/ppermute | solution.py:318
  19.4 6.0 %collective-permute-start.5 = (bf16[208,128]{1,0:T(8,128)(2,1)S(1)}, bf16[208,128]{1,0:T(8,128)(2,1)S(1)}, u32[]{:S(2)}, u32[]{:S(2)}) collective-permute-start(bf16[208,128]{1,0:T(8,128)(2,1)S(1)} %get-tuple-element.76), channel_id=1, source_target_pairs={{12,0},{0,4},{4,8},{8,12},{13,1},{1,5},{5,9},{9,13},{14,2},{2,6},{... | collective-permute-start | bytes 159752 | tf_op jit(solution)/shard_map/cond/branch_0_fun/ppermute | solution.py:250
  21.4 5.4 %collective-permute-start.4 = (bf16[400,128]{1,0:T(8,128)(2,1)S(1)}, bf16[400,128]{1,0:T(8,128)(2,1)S(1)}, u32[]{:S(2)}, u32[]{:S(2)}) collective-permute-start(bf16[400,128]{1,0:T(8,128)(2,1)S(1)} %get-tuple-element.75), channel_id=1, source_target_pairs={{0,1},{1,0},{2,3},{3,2},{4,5},{5,4},{6,7},{7,6},{8,9},{9,8},{10,11... | collective-permute-start | bytes 307208 | tf_op jit(solution)/shard_map/cond/branch_0_fun/ppermute | solution.py:254
  23.8 7.5 %collective-permute-start.8 = (bf16[400,128]{1,0:T(8,128)(2,1)S(1)}, bf16[400,128]{1,0:T(8,128)(2,1)S(1)}, u32[]{:S(2)}, u32[]{:S(2)}) collective-permute-start(bf16[400,128]{1,0:T(8,128)(2,1)S(1)} %branch_0_fun.20.one), channel_id=1, source_target_pairs={{0,8},{4,12},{8,0},{12,4},{1,9},{5,13},{9,1},{13,5},{2,10},{6,14},... | collective-permute-start | bytes 307208 | tf_op jit(solution)/shard_map/cond/branch_0_fun/ppermute | solution.py:318
  25.4 4.1 %collective-permute-start.6 = (bf16[208,128]{1,0:T(8,128)(2,1)S(1)}, bf16[208,128]{1,0:T(8,128)(2,1)S(1)}, u32[]{:S(2)}, u32[]{:S(2)}) collective-permute-start(bf16[208,128]{1,0:T(8,128)(2,1)S(1)} %collective-permute-done.5.far), channel_id=1, source_target_pairs={{0,2},{1,3},{2,0},{3,1},{4,6},{5,7},{6,4},{7,5},{8,10},{9,11},{10,... | collective-permute-start | bytes 159752 | tf_op jit(solution)/shard_map/cond/branch_0_fun/ppermute | solution.py:254
  31.6 1.8 %collective-permute-start.27 = (f32[400,256]{1,0:T(8,128)S(1)}, f32[400,256]{1,0:T(8,128)S(1)}, u32[]{:S(2)}, u32[]{:S(2)}) collective-permute-start(f32[400,256]{1,0:T(8,128)S(1)} %get-tuple-element.150.grads), channel_id=1, source_target_pairs={{0,1},{1,0},{2,3},{3,2},{4,5},{5,4},{6,7},{7,6},{8,9},{9,8},{10,11... | collective-permute-start | bytes 1228808 | tf_op jit(solution)/shard_map/ppermute | solution.py:254

commit v2 on v1

--- a/solution.py
+++ b/solution.py
@@ -114,7 +114,7 @@
 
 def edges_kernel(n_negs, far_half, far_rest, *refs):
     lists = (refs[0:4], refs[4:8])
-    lefts, keep, send, far, *totals = refs[8:]
+    lefts, keep, send, far_keep, far_send, far, *totals = refs[8:]
     mine, theirs = halves(far.shape[1])
     far[:, mine] = far_half[...]
     far[:, theirs] = far_rest[...]
@@ -166,11 +166,10 @@
             hot_total[...] = add_hot
         else:
             hot_total[...] += add_hot
-    cut = hot_rows // 2
+    outs = ((keep, send), (far_keep, far_send))
     for j, (mine, theirs) in enumerate((halves(hot_rows), halves(rows))):
-        lanes = slice(0, cut) if j == 0 else slice(cut, cut + rows // 2)
-        keep[:, lanes] = totals[j][:, mine] + totals[2 + j][:, mine]
-        send[:, lanes] = (totals[j][:, theirs] + totals[2 + j][:, theirs]).astype(BF)
+        outs[j][0][...] = totals[j][:, mine] + totals[2 + j][:, mine]
+        outs[j][1][...] = (totals[j][:, theirs] + totals[2 + j][:, theirs]).astype(BF)
 
 
 def own_kernel(ids_0, ids_1, lefts, far_in, keep, send, far, *totals):
@@ -191,12 +190,14 @@
     send[...] = (totals[0][:, theirs] + totals[1][:, theirs]).astype(BF)
 
 
-def pair_kernel(keep, got, hot, far):
-    cut = hot.shape[1]
-    hot[...] = (keep[:, :cut] + got[:, :cut].astype(F32)).astype(BF)
+def hot_pair_kernel(keep, got, hot):
+    hot[...] = (keep[...] + got[...].astype(F32)).astype(BF)
+
+
+def far_pair_kernel(keep, got, far):
     part = far.shape[0]
-    at = pl.ds(pl.multiple_of(lax.axis_index("rep") // 2 * (hot.shape[0] - part), 16), part)
-    far[...] = (keep[at, cut:] + got[at, cut:].astype(F32)).astype(BF)
+    at = pl.ds(pl.multiple_of(lax.axis_index("rep") // 2 * (keep.shape[0] - part), 16), part)
+    far[...] = (keep[at, :] + got[at, :].astype(F32)).astype(BF)
 
 
 def add_kernel(one, other, out):
@@ -291,16 +292,16 @@
     theirs = call(second_kernel, columns, n_in=3)(table, rel_parts, other)
     hot_half = struct((width, hot_rows // 2), BF)
     row_half = struct((width, rows // 2), BF)
-    both = (width, hot_rows // 2 + rows // 2)
-    lefts, keep, send = call(
+    lefts, keep, send, far_keep, far_send = call(
         functools.partial(edges_kernel, n_negs),
-        (struct((blocks, width, per), BF), struct(both, F32), struct(both, BF)),
+        (struct((blocks, width, per), BF), struct(hot_half.shape, F32), hot_half, struct(row_half.shape, F32), row_half),
         scratch=[pltpu.VMEM((width, rows), BF)]
         + [pltpu.VMEM((width, hot_rows), F32), pltpu.VMEM((width, rows), F32)] * 2,
         n_in=10,
     )(far_half, far_rest, ids, *mine, other, *theirs)
     part = struct((-(-width // 32) * 16, rows // 2), BF)
-    hot_sum, far_sum = call(pair_kernel, (hot_half, part), n_in=2)(keep, swapped(send, 1))
+    hot_sum = call(hot_pair_kernel, hot_half, n_in=2)(keep, swapped(send, 1))
+    far_sum = call(far_pair_kernel, part, n_in=2)(far_keep, swapped(far_send, 1))
     own_keep, own_send, far_sum = call(
         own_kernel,
         (struct(row_half.shape, F32), row_half, part),

time: 34 us -> 34.5 us (1.015); the launches traced: 34.4 us -> 34.1 us
    ppermute x6 -> x7, starting transfers between devices: 3.77 us -> 3.84 us  [swapped(): lax.ppermute(block, 'rep', [(i, i ^ bit) for i in range(lax.axis_size('re...]
    ppermute x6 -> x7, waiting for transfers between devices: 4.88 us -> 4.92 us  [swapped(): lax.ppermute(block, 'rep', [(i, i ^ bit) for i in range(lax.axis_size('re...]
  transfers between devices with their start and end apart: 10 -> 11, of which waited for: 7 -> 8; matrix products, arithmetic and copies ran while one was open for 0% -> 0% of each run, Pallas kernels for 18% -> 18%
where the time goes in v2:
time: 34.5 us; the launch traced here: 34.1 us
  starting transfers between devices  11.6 us (34%)
  Pallas kernels  11.1 us (32%)
  waiting for transfers between devices  9.8 us (28%)
  between operations  1.34 us (4%)
  loops' own time  0.35 us (1%)
    ppermute x2, starting transfers between devices, shifted(): lax.ppermute(block, axis, [((i - distance) % size, i) for i in range(size)])  6.93 us
    ppermute x7, waiting for transfers between devices, swapped(): lax.ppermute(block, 'rep', [(i, i ^ bit) for i in range(lax.axis_size('re...  4.92 us
    ppermute x7, starting transfers between devices, swapped(): lax.ppermute(block, 'rep', [(i, i ^ bit) for i in range(lax.axis_size('re...  3.84 us
    ppermute x2, waiting for transfers between devices, bucket(): hot_got = lax.ppermute(hot_sum, 'dom', route)  3.79 us
    pallas_call x1, Pallas kernels, bucket(): call(functools.partial(edges_kernel, n_negs), (struct((blocks, width, per...  2.7 us
    pallas_call x1, Pallas kernels, bucket(): call(first_kernel, (struct((width, rows + hot_rows), BF), struct((width,...  1.7 us
    pallas_call x1, Pallas kernels, bucket(): theirs = call(second_kernel, columns, n_in=3)(table, rel_parts, other)  1.69 us
    pallas_call x1, Pallas kernels, body(): call(near_update_kernel, (half, half_acc, half, half_acc), n_in=5)  1.26 us
  transfers between devices with their start and end apart: 11, of which 8 were waited for; matrix products, arithmetic and copies ran while one was open for 0% of the time, Pallas kernels for 18%

profile of v2, /device:TPU:0, one launch (start us, length us, event | category | flops | bytes accessed | tf_op | source)
XLA Modules:
  0.0 34.1 jit_solution(13576669803057118038)
XLA Ops:
  1.3 30.0 %conditional.1 = (f32[400,256]{1,0:T(8,128)S(1)}) conditional(s32[]{:T(128)} %clamp.3, (f32[400,256]{1,0:T(8,128)}, s32[1,1024]{1,0:T(1,128)}, s32[1,1024]{1,0:T(1,128)}, s32[1,1024]{1,0:T(1,128)}, s32[1,2,1000]{2,1,0:T(2,128)}, /*index=5*/f32[400,256]{1,0:T(8,128)}, f32[400,512]{1,0:T(8,128)}, s32[1]{0:T(128)}) %tuple.28, ...), branch_computations={%region_0.1_spmd, %region_1.2_spmd, %region_2.3_spmd} | conditional | flops 12 | bytes 9978360 | solution.py:336
  1.4 1.2 %branch_0_fun.12 = (bf16[400,128]{1,0:T(8,128)(2,1)S(1)}, s32[8,1024]{1,0:T(8,128)S(1)}) custom-call(f32[400,256]{1,0:T(8,128)} %get-tuple-element.39.emb, s32[1,1024]{1,0:T(1,128)} %get-tuple-element.54.lhs, s32[1,1024]{1,0:T(1,128)} %get-tuple-element.55.rhs, s32[1,1024]{1,0:T(1,128)} %get-tuple-element.56.rel, s32[1,2,1000]{2,1,0:T(2,128)} %get-tuple-element.57.neg, ...), custom_call_target="tpu_custom_call" | custom-call | flops 1 | bytes 1 | tf_op jit(solution)/shard_map/cond/branch_0_fun/pallas_call | solution.py:269
  2.6 5.1 %collective-permute-start.1 = (bf16[400,128]{1,0:T(8,128)(2,1)S(1)}, bf16[400,128]{1,0:T(8,128)(2,1)S(1)}, u32[]{:S(2)}, u32[]{:S(2)}) collective-permute-start(bf16[400,128]{1,0:T(8,128)(2,1)S(1)} %get-tuple-element.61), channel_id=1, source_target_pairs={{4,0},{8,4},{12,8},{0,12},{5,1},{9,5},{13,9},{1,13},{6,2},{10,6},{... | collective-permute-start | bytes 307208 | tf_op jit(solution)/shard_map/cond/branch_0_fun/ppermute | solution.py:251
  7.7 0.6 %branch_0_fun.13.ids.refs_0_.ids_0 = s32[8,1024]{1,0:T(8,128)S(1)} custom-call(s32[1]{0:T(128)} %get-tuple-element.38.count, s32[8,1024]{1,0:T(8,128)S(1)} %get-tuple-element.60.ids), custom_call_target="tpu_custom_call" | custom-call | flops 1 | bytes 1 | tf_op jit(solution)/shard_map/cond/branch_0_fun/pallas_call | solution.py:276
  8.3 1.6 %collective-permute-start = (s32[8,1024]{1,0:T(8,128)S(1)}, s32[8,1024]{1,0:T(8,128)S(1)}, u32[]{:S(2)}, u32[]{:S(2)}) collective-permute-start(s32[8,1024]{1,0:T(8,128)S(1)} %branch_0_fun.13.ids.refs_0_.ids_0), channel_id=1, source_target_pairs={{0,2},{1,3},{2,0},{3,1},{4,6},{5,7},{6,4},{7,5},{8,10},{9,11},{10,... | collective-permute-start | bytes 98312 | tf_op jit(solution)/shard_map/cond/branch_0_fun/ppermute | solution.py:255
  9.9 1.7 %branch_0_fun.14 = (bf16[400,512]{1,0:T(8,128)(2,1)S(1)}, bf16[400,1024]{1,0:T(8,128)(2,1)S(1)}, bf16[2,400,512]{2,1,0:T(8,128)(2,1)S(1)}, f32[2,400,512]{2,1,0:T(8,128)S(1)}, f32[2,256,128]{2,1,0:T(8,128)S(1)}) custom-call(f32[400,256]{1,0:T(8,128)S(1)} %copy-done.5, f32[400,256]{1,0:T(8,128)S(1)} %copy-done.8, f32[400,512]{1,0:T(8,128)S(1)} %copy-done.2, ...), custom_call_target="tpu_custom_call" | custom-call | flops 1 | bytes 1 | tf_op jit(solution)/shard_map/cond/branch_0_fun/pallas_call | solution.py:283
  11.6 0.7 %collective-permute-done.other.ids.refs_4_.ids_1 = s32[8,1024]{1,0:T(8,128)S(1)} collective-permute-done((s32[8,1024]{1,0:T(8,128)S(1)}, s32[8,1024]{1,0:T(8,128)S(1)}, u32[]{:S(2)}, u32[]{:S(2)}) %collective-permute-start) | collective-permute-done | bytes 32800 | tf_op jit(solution)/shard_map/cond/branch_0_fun/ppermute | solution.py:255
  12.4 1.7 %branch_0_fun.16 = (bf16[2,400,512]{2,1,0:T(8,128)(2,1)S(1)}, f32[2,400,512]{2,1,0:T(8,128)S(1)}, f32[2,256,128]{2,1,0:T(8,128)S(1)}) custom-call(bf16[400,512]{1,0:T(8,128)(2,1)S(1)} %get-tuple-element.62.after.table, bf16[400,1024]{1,0:T(8,128)(2,1)S(1)} %get-tuple-element.66.rel_parts, s32[8,1024]{1,0:T(8,128)S(1)} %collective-permute-done.other.ids.refs_4_.ids_1), custom_call_target="tpu_custom_call" | custom-call | flops 1 | bytes 1 | tf_op jit(solution)/shard_map/cond/branch_0_fun/pallas_call | solution.py:292
  14.1 2.7 %branch_0_fun.17 = (bf16[4,400,512]{2,1,0:T(8,128)(2,1)S(1)}, f32[400,128]{1,0:T(8,128)S(1)}, bf16[400,128]{1,0:T(8,128)(2,1)S(1)}, f32[400,128]{1,0:T(8,128)S(1)}, bf16[400,128]{1,0:T(8,128)(2,1)S(1)}) custom-call(bf16[400,128]{1,0:T(8,128)(2,1)S(1)} %branch_0_fun.15.far_half, bf16[400,128]{1,0:T(8,128)(2,1)S(1)} %collective-permute-done.2.far_rest, ...), custom_call_target="tpu_custom_call" | custom-call | flops 1 | bytes 1 | tf_op jit(solution)/shard_map/cond/branch_0_fun/pallas_call | solution.py:295
  16.8 0.6 %collective-permute-start.7 = (bf16[400,128]{1,0:T(8,128)(2,1)S(1)}, bf16[400,128]{1,0:T(8,128)(2,1)S(1)}, u32[]{:S(2)}, u32[]{:S(2)}) collective-permute-start(bf16[400,128]{1,0:T(8,128)(2,1)S(1)} %get-tuple-element.77), channel_id=1, source_target_pairs={{0,1},{1,0},{2,3},{3,2},{4,5},{5,4},{6,7},{7,6},{8,9},{9,8},{10,11... | collective-permute-start | bytes 307208 | tf_op jit(solution)/shard_map/cond/branch_0_fun/ppermute | solution.py:255
  17.4 0.9 %collective-permute-done.7.got = bf16[400,128]{1,0:T(8,128)(2,1)S(1)} collective-permute-done((bf16[400,128]{1,0:T(8,128)(2,1)S(1)}, bf16[400,128]{1,0:T(8,128)(2,1)S(1)}, u32[]{:S(2)}, u32[]{:S(2)}) %collective-permute-start.7) | collective-permute-done | bytes 102432 | tf_op jit(solution)/shard_map/cond/branch_0_fun/ppermute | solution.py:255
  18.4 0.3 collective-permute-done.3.got
  18.7 0.7 %branch_0_fun.19 = (f32[400,128]{1,0:T(8,128)S(1)}, bf16[400,128]{1,0:T(8,128)(2,1)S(1)}, bf16[208,128]{1,0:T(8,128)(2,1)S(1)}) custom-call(s32[8,1024]{1,0:T(8,128)S(1)} %branch_0_fun.13.ids.refs_0_.ids_0, s32[8,1024]{1,0:T(8,128)S(1)} %collective-permute-done.other.ids.refs_4_.ids_1, bf16[4,400,512]{2,1,0:T(8,128)(2,1)S(1)} %get-tuple-element.70.lefts, ...), custom_call_target="tpu_custom_call" | custom-call | flops 1 | bytes 1 | tf_op jit(solution)/shard_map/cond/branch_0_fun/pallas_call | solution.py:305
  19.4 1.8 %collective-permute-start.5 = (bf16[208,128]{1,0:T(8,128)(2,1)S(1)}, bf16[208,128]{1,0:T(8,128)(2,1)S(1)}, u32[]{:S(2)}, u32[]{:S(2)}) collective-permute-start(bf16[208,128]{1,0:T(8,128)(2,1)S(1)} %get-tuple-element.75), channel_id=1, source_target_pairs={{12,0},{0,4},{4,8},{8,12},{13,1},{1,5},{5,9},{9,13},{14,2},{2,6},{... | collective-permute-start | bytes 159752 | tf_op jit(solution)/shard_map/cond/branch_0_fun/ppermute | solution.py:251
  21.2 2.3 %collective-permute-done.8.other = bf16[400,128]{1,0:T(8,128)(2,1)S(1)} collective-permute-done((bf16[400,128]{1,0:T(8,128)(2,1)S(1)}, bf16[400,128]{1,0:T(8,128)(2,1)S(1)}, u32[]{:S(2)}, u32[]{:S(2)}) %collective-permute-start.8) | collective-permute-done | bytes 102432 | tf_op jit(solution)/shard_map/cond/branch_0_fun/ppermute | solution.py:319
  23.6 0.7 %collective-permute-start.9 = (bf16[400,128]{1,0:T(8,128)(2,1)S(1)}, bf16[400,128]{1,0:T(8,128)(2,1)S(1)}, u32[]{:S(2)}, u32[]{:S(2)}) collective-permute-start(bf16[400,128]{1,0:T(8,128)(2,1)S(1)} %branch_0_fun.22.one), channel_id=1, source_target_pairs={{0,8},{4,12},{8,0},{12,4},{1,9},{5,13},{9,1},{13,5},{2,10},{6,14},... | collective-permute-start | bytes 307208 | tf_op jit(solution)/shard_map/cond/branch_0_fun/ppermute | solution.py:319
  24.3 1.1 %collective-permute-done.5.far = bf16[208,128]{1,0:T(8,128)(2,1)S(1)} collective-permute-done((bf16[208,128]{1,0:T(8,128)(2,1)S(1)}, bf16[208,128]{1,0:T(8,128)(2,1)S(1)}, u32[]{:S(2)}, u32[]{:S(2)}) %collective-permute-start.5) | collective-permute-done | bytes 53280 | tf_op jit(solution)/shard_map/cond/branch_0_fun/ppermute | solution.py:251
  25.4 1.5 %collective-permute-start.6 = (bf16[208,128]{1,0:T(8,128)(2,1)S(1)}, bf16[208,128]{1,0:T(8,128)(2,1)S(1)}, u32[]{:S(2)}, u32[]{:S(2)}) collective-permute-start(bf16[208,128]{1,0:T(8,128)(2,1)S(1)} %collective-permute-done.5.far), channel_id=1, source_target_pairs={{0,2},{1,3},{2,0},{3,1},{4,6},{5,7},{6,4},{7,5},{8,10},{9,11},{10,... | collective-permute-start | bytes 159752 | tf_op jit(solution)/shard_map/cond/branch_0_fun/ppermute | solution.py:255
  26.9 2.6 %collective-permute-done.6.far_other = bf16[208,128]{1,0:T(8,128)(2,1)S(1)} collective-permute-done((bf16[208,128]{1,0:T(8,128)(2,1)S(1)}, bf16[208,128]{1,0:T(8,128)(2,1)S(1)}, u32[]{:S(2)}, u32[]{:S(2)}) %collective-permute-start.6) | collective-permute-done | bytes 53280 | tf_op jit(solution)/shard_map/cond/branch_0_fun/ppermute | solution.py:255
  29.6 1.5 %collective-permute-done.9.other = bf16[400,128]{1,0:T(8,128)(2,1)S(1)} collective-permute-done((bf16[400,128]{1,0:T(8,128)(2,1)S(1)}, bf16[400,128]{1,0:T(8,128)(2,1)S(1)}, u32[]{:S(2)}, u32[]{:S(2)}) %collective-permute-start.9) | collective-permute-done | bytes 102432 | tf_op jit(solution)/shard_map/cond/branch_0_fun/ppermute | solution.py:319
  31.3 0.1 collective-permute-start.30
  31.4 1.3 %shard_map.138 = (f32[400,256]{1,0:T(8,128)S(1)}, f32[1,256]{1,0:T(1,128)S(1)}, f32[400,256]{1,0:T(8,128)S(1)}, f32[1,256]{1,0:T(1,128)S(1)}) custom-call(f32[400,256]{1,0:T(8,128)S(1)} %get-tuple-element.150.grads, f32[400,256]{1,0:T(8,128)} %bitcast.19, f32[1,256]{1,0:T(1,128)S(1)} %bitcast.11, f32[400,256]{1,0:T(8,128)} %bitcast.23, f32[1,256]{1,0:T(1,128)S(1)} %bitcast.12), custom_call_target="tpu_custom_call" | custom-call | flops 1 | bytes 1 | tf_op jit(solution)/shard_map/pallas_call | solution.py:369
  32.7 0.4 %collective-permute-done.30.grads = f32[400,256]{1,0:T(8,128)S(1)} collective-permute-done((f32[400,256]{1,0:T(8,128)S(1)}, f32[400,256]{1,0:T(8,128)S(1)}, u32[]{:S(2)}, u32[]{:S(2)}) %collective-permute-start.30) | collective-permute-done | bytes 409632 | tf_op jit(solution)/shard_map/ppermute | solution.py:255
  33.1 1.0 %shard_map.139 = (f32[400,256]{1,0:T(8,128)}, f32[1,256]{1,0:T(1,128)}, f32[400,256]{1,0:T(8,128)}, f32[1,256]{1,0:T(1,128)}) custom-call(f32[400,256]{1,0:T(8,128)S(1)} %collective-permute-done.30.grads, f32[400,256]{1,0:T(8,128)S(1)} %get-tuple-element.142.done, f32[1,256]{1,0:T(1,128)S(1)} %get-tuple-element.143.done_acc, ...), custom_call_target="tpu_custom_call" | custom-call | flops 1 | bytes 1 | tf_op jit(solution)/shard_map/pallas_call | solution.py:372
  (23 shorter events, 0.4 us)
Async XLA Ops:
  1.3 30.1 %copy-start = (f32[256]{0:T(256)S(1)}, f32[256]{0:T(256)}, u32[]{:S(2)}) copy-start(f32[256]{0:T(256)} %param.21) | copy-start | bytes 3076
  1.3 30.1 %copy-start.1 = (f32[256]{0:T(256)S(1)}, f32[256]{0:T(256)}, u32[]{:S(2)}) copy-start(f32[256]{0:T(256)} %param.23) | copy-start | bytes 3076
  1.3 8.5 %copy-start.2 = (f32[400,512]{1,0:T(8,128)S(1)}, f32[400,512]{1,0:T(8,128)}, u32[]{:S(2)}) copy-start(f32[400,512]{1,0:T(8,128)} %get-tuple-element.59.relations.rel) | copy-start | bytes 2457604 | tf_op jit(solution)/shard_map/cond
  1.3 8.5 %copy-start.5 = (f32[400,256]{1,0:T(8,128)S(1)}, f32[400,256]{1,0:T(8,128)}, u32[]{:S(2)}) copy-start(f32[400,256]{1,0:T(8,128)} %get-tuple-element.39.emb) | copy-start | bytes 1228804 | tf_op jit(solution)/shard_map/cond
  1.4 8.5 %copy-start.8 = (f32[400,256]{1,0:T(8,128)S(1)}, f32[400,256]{1,0:T(8,128)}, u32[]{:S(2)}) copy-start(f32[400,256]{1,0:T(8,128)} %get-tuple-element.58.hot) | copy-start | bytes 1228804 | tf_op jit(solution)/shard_map/cond
  2.6 9.7 %collective-permute-start.1 = (bf16[400,128]{1,0:T(8,128)(2,1)S(1)}, bf16[400,128]{1,0:T(8,128)(2,1)S(1)}, u32[]{:S(2)}, u32[]{:S(2)}) collective-permute-start(bf16[400,128]{1,0:T(8,128)(2,1)S(1)} %get-tuple-element.61), channel_id=1, source_target_pairs={{4,0},{8,4},{12,8},{0,12},{5,1},{9,5},{13,9},{1,13},{6,2},{10,6},{... | collective-permute-start | bytes 307208 | tf_op jit(solution)/shard_map/cond/branch_0_fun/ppermute | solution.py:251
  8.3 4.0 %collective-permute-start = (s32[8,1024]{1,0:T(8,128)S(1)}, s32[8,1024]{1,0:T(8,128)S(1)}, u32[]{:S(2)}, u32[]{:S(2)}) collective-permute-start(s32[8,1024]{1,0:T(8,128)S(1)} %branch_0_fun.13.ids.refs_0_.ids_0), channel_id=1, source_target_pairs={{0,2},{1,3},{2,0},{3,1},{4,6},{5,7},{6,4},{7,5},{8,10},{9,11},{10,... | collective-permute-start | bytes 98312 | tf_op jit(solution)/shard_map/cond/branch_0_fun/ppermute | solution.py:255
  12.3 1.8 %collective-permute-start.2 = (bf16[400,128]{1,0:T(8,128)(2,1)S(1)}, bf16[400,128]{1,0:T(8,128)(2,1)S(1)}, u32[]{:S(2)}, u32[]{:S(2)}) collective-permute-start(bf16[400,128]{1,0:T(8,128)(2,1)S(1)} %branch_0_fun.15.far_half), channel_id=1, source_target_pairs={{0,1},{1,0},{2,3},{3,2},{4,5},{5,4},{6,7},{7,6},{8,9},{9,8},{10,11... | collective-permute-start | bytes 307208 | tf_op jit(solution)/shard_map/cond/branch_0_fun/ppermute | solution.py:255
  16.8 1.5 %collective-permute-start.7 = (bf16[400,128]{1,0:T(8,128)(2,1)S(1)}, bf16[400,128]{1,0:T(8,128)(2,1)S(1)}, u32[]{:S(2)}, u32[]{:S(2)}) collective-permute-start(bf16[400,128]{1,0:T(8,128)(2,1)S(1)} %get-tuple-element.77), channel_id=1, source_target_pairs={{0,1},{1,0},{2,3},{3,2},{4,5},{5,4},{6,7},{7,6},{8,9},{9,8},{10,11... | collective-permute-start | bytes 307208 | tf_op jit(solution)/shard_map/cond/branch_0_fun/ppermute | solution.py:255
  17.4 1.3 %collective-permute-start.3 = (bf16[400,128]{1,0:T(8,128)(2,1)S(1)}, bf16[400,128]{1,0:T(8,128)(2,1)S(1)}, u32[]{:S(2)}, u32[]{:S(2)}) collective-permute-start(bf16[400,128]{1,0:T(8,128)(2,1)S(1)} %get-tuple-element.72), channel_id=1, source_target_pairs={{0,1},{1,0},{2,3},{3,2},{4,5},{5,4},{6,7},{7,6},{8,9},{9,8},{10,11... | collective-permute-start | bytes 307208 | tf_op jit(solution)/shard_map/cond/branch_0_fun/ppermute | solution.py:255
  18.3 5.2 %collective-permute-start.8 = (bf16[400,128]{1,0:T(8,128)(2,1)S(1)}, bf16[400,128]{1,0:T(8,128)(2,1)S(1)}, u32[]{:S(2)}, u32[]{:S(2)}) collective-permute-start(bf16[400,128]{1,0:T(8,128)(2,1)S(1)} %branch_0_fun.21.one), channel_id=1, source_target_pairs={{0,4},{4,0},{8,12},{12,8},{1,5},{5,1},{9,13},{13,9},{2,6},{6,2},{1... | collective-permute-start | bytes 307208 | tf_op jit(solution)/shard_map/cond/branch_0_fun/ppermute | solution.py:319
  19.4 6.0 %collective-permute-start.5 = (bf16[208,128]{1,0:T(8,128)(2,1)S(1)}, bf16[208,128]{1,0:T(8,128)(2,1)S(1)}, u32[]{:S(2)}, u32[]{:S(2)}) collective-permute-start(bf16[208,128]{1,0:T(8,128)(2,1)S(1)} %get-tuple-element.75), channel_id=1, source_target_pairs={{12,0},{0,4},{4,8},{8,12},{13,1},{1,5},{5,9},{9,13},{14,2},{2,6},{... | collective-permute-start | bytes 159752 | tf_op jit(solution)/shard_map/cond/branch_0_fun/ppermute | solution.py:251
  21.2 5.6 %collective-permute-start.4 = (bf16[400,128]{1,0:T(8,128)(2,1)S(1)}, bf16[400,128]{1,0:T(8,128)(2,1)S(1)}, u32[]{:S(2)}, u32[]{:S(2)}) collective-permute-start(bf16[400,128]{1,0:T(8,128)(2,1)S(1)} %get-tuple-element.74), channel_id=1, source_target_pairs={{0,1},{1,0},{2,3},{3,2},{4,5},{5,4},{6,7},{7,6},{8,9},{9,8},{10,11... | collective-permute-start | bytes 307208 | tf_op jit(solution)/shard_map/cond/branch_0_fun/ppermute | solution.py:255
  23.6 7.4 %collective-permute-start.9 = (bf16[400,128]{1,0:T(8,128)(2,1)S(1)}, bf16[400,128]{1,0:T(8,128)(2,1)S(1)}, u32[]{:S(2)}, u32[]{:S(2)}) collective-permute-start(bf16[400,128]{1,0:T(8,128)(2,1)S(1)} %branch_0_fun.22.one), channel_id=1, source_target_pairs={{0,8},{4,12},{8,0},{12,4},{1,9},{5,13},{9,1},{13,5},{2,10},{6,14},... | collective-permute-start | bytes 307208 | tf_op jit(solution)/shard_map/cond/branch_0_fun/ppermute | solution.py:319
  25.4 4.1 %collective-permute-start.6 = (bf16[208,128]{1,0:T(8,128)(2,1)S(1)}, bf16[208,128]{1,0:T(8,128)(2,1)S(1)}, u32[]{:S(2)}, u32[]{:S(2)}) collective-permute-start(bf16[208,128]{1,0:T(8,128)(2,1)S(1)} %collective-permute-done.5.far), channel_id=1, source_target_pairs={{0,2},{1,3},{2,0},{3,1},{4,6},{5,7},{6,4},{7,5},{8,10},{9,11},{10,... | collective-permute-start | bytes 159752 | tf_op jit(solution)/shard_map/cond/branch_0_fun/ppermute | solution.py:255
  31.3 1.8 %collective-permute-start.30 = (f32[400,256]{1,0:T(8,128)S(1)}, f32[400,256]{1,0:T(8,128)S(1)}, u32[]{:S(2)}, u32[]{:S(2)}) collective-permute-start(f32[400,256]{1,0:T(8,128)S(1)} %get-tuple-element.150.grads), channel_id=1, source_target_pairs={{0,1},{1,0},{2,3},{3,2},{4,5},{5,4},{6,7},{7,6},{8,9},{9,8},{10,11... | collective-permute-start | bytes 1228808 | tf_op jit(solution)/shard_map/ppermute | solution.py:255
